TPU v7x, 128 devices: a whole 4x4x4 slice. The times are simulated.
128 devices in a mesh: lon: 16 (over x, y), lat: 8 (over z, core).
Axes of the slice: x: 4, y: 4, z: 4, core: 2. Of those that a mesh axis runs over, the one named last changes fastest.
Arguments:
- checkpoint: float32 [8, 512, 9600], P('lat', 'lon'), may hold values from -6 to 6
- slot_dest: int32 [8, 512], P('lat'), may hold values from -1 to 511, as said below
- kmt: int32 [1280, 7680], P('lat', 'lon'), may hold values from 0 to 2, as said below
- kappa: float32 [2, 1280, 7680], P(None, 'lat', 'lon'), may hold values from 0.02 to 0.2
Outputs:
- new_tracer: float32 [2, 2, 1280, 7680], P(None, None, 'lat', 'lon')
- stream: float32 [1280, 7680], P('lat', 'lon')
Inputs may be any that keep to these rules, and one draw needn't show every extreme that they name: `slot_dest`: in each band every value e * 32 + p is named by at most one slot; at most 2 slots of one checkpoint owner's 32 slots name one new owner e, and exactly 2 for some pair in every band. Positions that no slot names are land blocks. kmt is 0 on every point of a land block.
All inputs are finite; a program needn't handle non-finite values.
Results may differ from a plain program's by a relative error of at most 0.0001.
Values sent between devices are 32-bit elements; how exact they have to be, the bound alone decides.
A program may use at most 128 MiB of HBM per device.

v0:
```python
import jax
import jax.numpy as jnp
from jax import lax
from jax.sharding import PartitionSpec as P

BH = 40
BW = 60
LEV = 2
ITERS = 3


thermal = 0.25
haline = 0.75
cabbeling = 0.05


def extended(value, sides, width, wrap):
    for axis, dim in sides:
        size, length = (lax.axis_size(axis), value.shape[dim])
        up = [(i, (i + 1) % size) for i in range(size if wrap else size - 1)]
        down = [(j, i) for i, j in up]
        last = lax.slice_in_dim(value, length - width, length, axis=dim)
        initial = lax.slice_in_dim(value, 0, width, axis=dim)
        before = lax.ppermute(last, axis, up)
        after = lax.ppermute(initial, axis, down)
        value = jnp.concatenate([before, value, after], axis=dim)
    return value


def extend(field):
    beside_all = extended(field, (("lon", 2),), 1, True)
    return extended(beside_all, (("lat", 1),), 1, False)


def operate(vector, depth, column):
    wide = extend(vector[None])[0]
    edges = wide[2:, 1:-1] + wide[:-2, 1:-1] + wide[1:-1, 2:] + wide[1:-1, :-2]
    corners = wide[2:, 2:] + wide[2:, :-2] + wide[:-2, 2:] + wide[:-2, :-2]
    return column * ((6.0 + depth) * vector - edges - 0.5 * corners)


def squares(residual):
    return lax.psum(jnp.sum(residual * residual), ("lon", "lat"))


def body(checkpoint, slot_dest, kmt, kappa):
    myself = lax.axis_index("lon")
    blocks = checkpoint[0]
    dest_all = slot_dest[0]
    slots_dev = blocks.shape[0]
    values_blk = blocks.shape[1]
    owner = jnp.where(dest_all >= 0, dest_all // slots_dev, -1)
    landing = jnp.where(dest_all >= 0, dest_all % slots_dev, 0)
    empty = jnp.zeros((slots_dev + 1, values_blk), jnp.float32)
    target = jnp.where(owner == myself, landing, slots_dev)
    placed = empty.at[target].set(lax.all_gather(blocks, "lon", axis=0, tiled=True))[:slots_dev]
    rows_dev = kmt.shape[0]
    cols_dev = kmt.shape[1]
    block_rows = rows_dev // BH
    block_cols = cols_dev // BW
    field = placed.reshape(block_rows, block_cols, 2, LEV, BH, BW)
    field = field.transpose(2, 3, 0, 4, 1, 5).reshape(2, LEV, rows_dev, cols_dev)
    levels = jnp.arange(LEV, dtype=jnp.int32)
    wet = (levels[:, None, None] < kmt[None]).astype(jnp.float32)
    tracer = field * wet
    stacked = jnp.concatenate([tracer.reshape(2 * LEV, rows_dev, cols_dev), wet, kappa], axis=0)
    wide = extend(stacked)
    tracer_w = wide[: 2 * LEV].reshape(2, LEV, rows_dev + 2, cols_dev + 2)
    wet_w = wide[2 * LEV : 3 * LEV]
    kappa_w = wide[3 * LEV :]
    tracer_c = tracer_w[..., 1:-1, 1:-1]
    wet_c = wet_w[:, 1:-1, 1:-1]
    kappa_c = kappa_w[:, 1:-1, 1:-1]
    change = jnp.zeros_like(tracer)
    for step_y, step_x in ((0, 1), (0, -1), (1, 0), (-1, 0)):
        rows = slice(1 + step_y, 1 + step_y + rows_dev)
        cols = slice(1 + step_x, 1 + step_x + cols_dev)
        face = 0.5 * (kappa_c + kappa_w[:, rows, cols]) * wet_c * wet_w[:, rows, cols]
        change = change + face * (tracer_w[..., rows, cols] - tracer_c)
    new_tracer = wet * (tracer + change)
    thickness = 1.0 + 0.5 * jnp.arange(LEV, dtype=jnp.float32)
    temp = new_tracer[0]
    salt = new_tracer[1]
    density = wet * (haline * salt - thermal * temp - cabbeling * temp * temp)
    forcing = jnp.sum(thickness[:, None, None] * density, axis=0)
    depth = jnp.sum(thickness[:, None, None] * wet, axis=0)
    column = (kmt > 0).astype(jnp.float32)
    stream = jnp.zeros_like(forcing)
    residual = column * forcing
    direction = residual
    norm_now = squares(residual)
    for step in range(ITERS):
        image = operate(direction, depth, column)
        alpha = norm_now / lax.psum(jnp.sum(direction * image), ("lon", "lat"))
        stream = stream + alpha * direction
        residual = residual - alpha * image
        norm_next = squares(residual)
        direction = residual + norm_next / norm_now * direction
        norm_now = norm_next
    return (new_tracer, stream)


def solution(mesh):
    placed = (P("lat", "lon", None), P("lat", None), P("lat", "lon"), P(None, "lat", "lon"))
    return jax.shard_map(
        body,
        mesh=mesh,
        in_specs=placed,
        out_specs=(P(None, None, "lat", "lon"), P("lat", "lon")),
        check_vma=False,
    )
```

profile of v0, /device:TPU:1, one launch (start us, length us, event | category | flops | bytes accessed | tf_op | source)
XLA Modules:
  0.0 587.6 jit_solution(797138567132245220)
XLA Ops:
  7.2 0.7 all-gather.3.cloned.1.call-update
  7.9 0.7 compare_select_fusion
  8.6 0.1 fusion.30
  8.7 130.6 %all-gather.3.cloned.1.call-done = f32[1,512,9600]{2,1,0:T(8,128)} async-done(((f32[1,32,9600]{2,1,0:T(8,128)}), f32[1,512,9600]{2,1,0:T(8,128)}) %all-gather.3.cloned.1.call-update) | async-done | bytes 19660816 | tf_op jit(solution)/shard_map/all_gather | solution.py:56
  139.3 18.8 %scatter_custom_fusion = f32[33,9600]{1,0:T(8,128)S(1)} fusion(s32[512]{0:T(512)S(1)} %bitcast.51, f32[1,512,9600]{2,1,0:T(8,128)} %all-gather.3.cloned.1.call-done, f32[]{:T(128)} %constant.51.clone.1), kind=kCustom, calls=%fused_computation.1 | custom fusion | bytes 20928004 | tf_op jit(solution)/shard_map/scatter | solution.py:56
  158.2 0.1 slice.258
  158.3 5.4 reshape.159
  163.7 3.3 copy.8
  167.0 1.5 copy-done
  168.5 1.7 reshape.161
  170.2 1.6 bitcast_multiply_fusion
  171.8 0.2 pad_maximum_fusion.19
  172.1 0.3 copy.12
  172.4 0.3 copy.10
  172.7 2.8 collective-permute-start
  175.5 2.9 reshape.160
  178.5 2.9 collective-permute-done.1
  181.3 0.3 copy.13
  181.6 0.3 copy.11
  182.0 1.0 pad_maximum_fusion.29
  183.0 4.0 collective-permute-start.3
  187.0 0.8 fusion.27
  187.9 3.1 collective-permute-start.2
  191.0 0.4 fusion.21
  191.3 0.5 collective-permute-done.2
  191.8 0.4 fusion.18
  192.2 0.5 pad_maximum_fusion
  192.7 0.8 copy-done.6
  193.5 1.4 fusion.5
  194.9 0.3 select_reduce_fusion
  195.3 0.7 copy-done.5
  196.0 0.1 fusion.50
  196.1 4.8 collective-permute-start.5
  200.9 2.5 collective-permute-done.4
  203.5 4.6 collective-permute-start.6
  208.2 1.9 collective-permute-start.7
  210.1 3.0 collective-permute-done.7
  213.1 0.2 maximum_bitcast_fusion
  213.3 1.1 multiply_reduce_fusion.3
  214.4 65.6 %all-reduce = (f32[]{:T(128)}, f32[]{:T(128)}) all-reduce(f32[]{:T(128)} %get-tuple-element.3, f32[]{:T(128)} %get-tuple-element.2), channel_id=1, replica_groups=mesh['lon'=16,'lat'=8] {'lon','lat'}, use_global_device_ids=true, to_apply=%region_3.4 | all-reduce | flops 2 | bytes 16 | tf_op jit(solution)/shard_map/psum | solution.py:43
  281.3 0.7 multiply_reduce_fusion.2
  282.0 63.5 %psum.44 = f32[]{:T(128)} all-reduce(f32[]{:T(128)} %get-tuple-element.10), channel_id=1, replica_groups=mesh['lon'=16,'lat'=8] {'lon','lat'}, use_global_device_ids=true, to_apply=%region_8.9 | all-reduce | flops 1 | bytes 8 | tf_op jit(solution)/shard_map/psum | solution.py:43
  346.9 0.1 fusion.49
  347.1 4.8 collective-permute-start.9
  351.9 1.8 collective-permute-done.8
  353.8 4.3 collective-permute-start.10
  358.1 1.9 collective-permute-start.11
  360.0 3.0 collective-permute-done.11
  363.0 0.2 maximum_bitcast_fusion.1
  363.2 1.1 multiply_reduce_fusion.1
  364.3 65.3 %psum.45 = f32[]{:T(128)} all-reduce(f32[]{:T(128)} %get-tuple-element.8), channel_id=1, replica_groups=mesh['lon'=16,'lat'=8] {'lon','lat'}, use_global_device_ids=true, to_apply=%region_10.11 | all-reduce | flops 1 | bytes 8 | tf_op jit(solution)/shard_map/psum | solution.py:94
  430.9 0.7 multiply_reduce_fusion
  431.5 63.5 %psum.46 = f32[]{:T(128)} all-reduce(f32[]{:T(128)} %multiply_reduce_fusion), channel_id=1, replica_groups=mesh['lon'=16,'lat'=8] {'lon','lat'}, use_global_device_ids=true, to_apply=%region_12.13 | all-reduce | flops 1 | bytes 8 | tf_op jit(solution)/shard_map/psum | solution.py:43
  496.3 0.1 multiply_add_fusion.1
  496.4 0.1 fusion.48
  496.6 4.8 collective-permute-start.13
  501.4 1.8 collective-permute-done.12
  503.3 4.4 collective-permute-start.14
  507.7 1.9 collective-permute-start.15
  509.7 3.0 collective-permute-done.15
  512.6 0.2 maximum_bitcast_fusion.2
  512.8 1.1 fusion.35
  513.9 64.8 %psum.47 = f32[]{:T(128)} all-reduce(f32[]{:T(128)} %fusion.35), channel_id=1, replica_groups=mesh['lon'=16,'lat'=8] {'lon','lat'}, use_global_device_ids=true, to_apply=%region_14.15 | all-reduce | flops 1 | bytes 8 | tf_op jit(solution)/shard_map/psum | solution.py:94
  579.9 0.8 multiply_add_fusion
  (30 shorter events, 0.7 us)
Async XLA Ops:
  7.2 1.5 copy-start.3
  7.2 132.2 %all-gather.3.cloned.1.call-start = ((), (), s32[]{:S(2)}) async-start(), calls=%async_computation | async-start | bytes 20889600 | tf_op jit(solution)/shard_map/all_gather | solution.py:56
  167.0 1.5 copy-start
  170.2 1.6 copy-start.1
  172.7 8.9 %collective-permute-start = (f32[8,160,1]{1,0,2:T(8,128)S(1)}, f32[8,160,1]{1,0,2:T(8,128)S(1)}, u32[]{:S(2)}, u32[]{:S(2)}) collective-permute-start(f32[8,160,1]{1,0,2:T(8,128)S(1)} %copy.10), channel_id=1, source_target_pairs={{8,0},{16,8},{24,16},{32,24},{40,32},{48,40},{56,48},{64,56},{72,6... | collective-permute-start | bytes 15368 | tf_op jit(solution)/shard_map/ppermute | solution.py:25
  175.5 5.8 collective-permute-start.1
  181.9 5.1 copy-start.2
  181.9 5.1 copy-start.4
  183.0 8.0 %collective-permute-start.3 = (f32[8,1,482]{2,1,0:T(1,128)S(1)}, f32[8,1,482]{2,1,0:T(1,128)S(1)}, u32[]{:S(2)}, u32[]{:S(2)}) collective-permute-start(f32[8,1,482]{2,1,0:T(1,128)S(1)} %get-tuple-element.16), channel_id=1, source_target_pairs={{1,0},{2,1},{3,2},{4,3},{5,4},{6,5},{7,6},{9,8},{10,9},{11,10},{12... | collective-permute-start | bytes 46280 | tf_op jit(solution)/shard_map/ppermute | solution.py:25
  187.9 3.9 collective-permute-start.2
  192.2 1.3 copy-start.6
  194.9 1.1 copy-start.5
  196.1 7.4 %collective-permute-start.4 = (f32[1,160,1]{2,1,0:T(8,128)S(1)}, f32[1,160,1]{2,1,0:T(8,128)S(1)}, u32[]{:S(2)}, u32[]{:S(2)}) collective-permute-start(f32[1,160,1]{2,1,0:T(8,128)S(1)} %get-tuple-element.31), channel_id=1, source_target_pairs={{0,8},{8,16},{16,24},{24,32},{32,40},{40,48},{48,56},{56,64},{64,7... | collective-permute-start | bytes 1928 | tf_op jit(solution)/shard_map/ppermute | solution.py:24
  196.1 7.3 %collective-permute-start.5 = (f32[1,160,1]{2,1,0:T(8,128)S(1)}, f32[1,160,1]{2,1,0:T(8,128)S(1)}, u32[]{:S(2)}, u32[]{:S(2)}) collective-permute-start(f32[1,160,1]{2,1,0:T(8,128)S(1)} %get-tuple-element.32), channel_id=1, source_target_pairs={{8,0},{16,8},{24,16},{32,24},{40,32},{48,40},{56,48},{64,56},{72,6... | collective-permute-start | bytes 1928 | tf_op jit(solution)/shard_map/ppermute | solution.py:25
  203.5 6.6 %collective-permute-start.6 = (f32[1,1,482]{2,1,0:T(1,128)S(1)}, f32[1,1,482]{2,1,0:T(1,128)S(1)}, u32[]{:S(2)}, u32[]{:S(2)}) collective-permute-start(f32[1,1,482]{2,1,0:T(1,128)S(1)} %get-tuple-element.25), channel_id=1, source_target_pairs={{0,1},{1,2},{2,3},{3,4},{4,5},{5,6},{6,7},{8,9},{9,10},{10,11},{11... | collective-permute-start | bytes 5792 | tf_op jit(solution)/shard_map/ppermute | solution.py:24
  208.2 4.9 collective-permute-start.7
  347.0 6.7 %collective-permute-start.8 = (f32[1,160,1]{2,1,0:T(8,128)S(1)}, f32[1,160,1]{2,1,0:T(8,128)S(1)}, u32[]{:S(2)}, u32[]{:S(2)}) collective-permute-start(f32[1,160,1]{2,1,0:T(8,128)S(1)} %get-tuple-element.29), channel_id=1, source_target_pairs={{0,8},{8,16},{16,24},{24,32},{32,40},{40,48},{48,56},{56,64},{64,7... | collective-permute-start | bytes 1928 | tf_op jit(solution)/shard_map/ppermute | solution.py:24
  347.1 6.6 %collective-permute-start.9 = (f32[1,160,1]{2,1,0:T(8,128)S(1)}, f32[1,160,1]{2,1,0:T(8,128)S(1)}, u32[]{:S(2)}, u32[]{:S(2)}) collective-permute-start(f32[1,160,1]{2,1,0:T(8,128)S(1)} %get-tuple-element.30), channel_id=1, source_target_pairs={{8,0},{16,8},{24,16},{32,24},{40,32},{48,40},{56,48},{64,56},{72,6... | collective-permute-start | bytes 1928 | tf_op jit(solution)/shard_map/ppermute | solution.py:25
  353.8 6.2 %collective-permute-start.10 = (f32[1,1,482]{2,1,0:T(1,128)S(1)}, f32[1,1,482]{2,1,0:T(1,128)S(1)}, u32[]{:S(2)}, u32[]{:S(2)}) collective-permute-start(f32[1,1,482]{2,1,0:T(1,128)S(1)} %get-tuple-element.23), channel_id=1, source_target_pairs={{0,1},{1,2},{2,3},{3,4},{4,5},{5,6},{6,7},{8,9},{9,10},{10,11},{11... | collective-permute-start | bytes 5792 | tf_op jit(solution)/shard_map/ppermute | solution.py:24
  358.1 4.9 collective-permute-start.11
  496.5 6.7 %collective-permute-start.12 = (f32[1,160,1]{2,1,0:T(8,128)S(1)}, f32[1,160,1]{2,1,0:T(8,128)S(1)}, u32[]{:S(2)}, u32[]{:S(2)}) collective-permute-start(f32[1,160,1]{2,1,0:T(8,128)S(1)} %get-tuple-element.27), channel_id=1, source_target_pairs={{0,8},{8,16},{16,24},{24,32},{32,40},{40,48},{48,56},{56,64},{64,7... | collective-permute-start | bytes 1928 | tf_op jit(solution)/shard_map/ppermute | solution.py:24
  496.6 6.6 %collective-permute-start.13 = (f32[1,160,1]{2,1,0:T(8,128)S(1)}, f32[1,160,1]{2,1,0:T(8,128)S(1)}, u32[]{:S(2)}, u32[]{:S(2)}) collective-permute-start(f32[1,160,1]{2,1,0:T(8,128)S(1)} %get-tuple-element.28), channel_id=1, source_target_pairs={{8,0},{16,8},{24,16},{32,24},{40,32},{48,40},{56,48},{64,56},{72,6... | collective-permute-start | bytes 1928 | tf_op jit(solution)/shard_map/ppermute | solution.py:25
  503.3 6.4 %collective-permute-start.14 = (f32[1,1,482]{2,1,0:T(1,128)S(1)}, f32[1,1,482]{2,1,0:T(1,128)S(1)}, u32[]{:S(2)}, u32[]{:S(2)}) collective-permute-start(f32[1,1,482]{2,1,0:T(1,128)S(1)} %get-tuple-element.21), channel_id=1, source_target_pairs={{0,1},{1,2},{2,3},{3,4},{4,5},{5,6},{6,7},{8,9},{9,10},{10,11},{11... | collective-permute-start | bytes 5792 | tf_op jit(solution)/shard_map/ppermute | solution.py:24
  507.7 4.9 collective-permute-start.15
Sparse Core Ops, SparseCore 0:
  10.2 129.0 all-gather.2
where the time goes:
time: 589 us; the launch traced here: 588 us
  blocking collectives  323 us (55%)
  waiting for transfers between devices  150 us (25%)
  starting transfers between devices  43.6 us (7%)
  local copies, waits for them, and re-layouts  36.8 us (6%)
  between operations  20.9 us (4%)
  other arithmetic  14 us (2%)
    psum x3, blocking collectives, squares(): return lax.psum(jnp.sum(residual * residual), ('lon', 'lat'))  193 us
    all_gather x1, waiting for transfers between devices, body(): lax.all_gather(blocks, 'lon', axis=0, tiled=True)  131 us
    psum x2, blocking collectives, body(): alpha = norm_now / lax.psum(jnp.sum(direction * image), ('lon', 'lat'))  130 us
    ppermute x8, starting transfers between devices, extended(): after = lax.ppermute(initial, axis, down)  26.9 us
    scatter x1, local copies, waits for them, and re-layouts, body(): empty.at[target].set(lax.all_gather(blocks, 'lon', axis=0, tiled=True))  18.8 us
    ppermute x8, starting transfers between devices, extended(): before = lax.ppermute(last, axis, up)  16.7 us
  transfers between devices with their start and end apart: 17, of which 9 were waited for; matrix products, arithmetic and copies ran while one was open for 1% of the time, Pallas kernels for 0%

commit v1 on v0

v1 whole, which is shorter than its diff:
```python
import jax
import jax.numpy as jnp
from jax import lax
from jax.experimental import pallas as pl
from jax.experimental.pallas import tpu as pltpu
from jax.sharding import PartitionSpec as P

BW = 60
BH = 40
BX = 8
BY = 4
Q = 32
ROWS = 160
COLS = 480
NLON = 16
NLAT = 8
SIDE = 4
TILES = 21
SHIFT = 6.0
CHUNK = 1920

thermal = 0.25
haline = 0.75
cabbeling = 0.05

f32 = jnp.float32


def owners(dest, me):
    dest = dest.reshape(NLON, Q)
    own = dest >> 5
    slot = jnp.arange(Q, dtype=jnp.int32)
    mine = lax.dynamic_index_in_dim(own, me, 0, keepdims=False)
    goes = mine[None] == jnp.arange(NLON, dtype=jnp.int32)[:, None]
    one = jnp.min(jnp.where(goes, slot, Q - 1), axis=1)
    two = jnp.max(jnp.where(goes, slot, 0), axis=1)
    first = jnp.min(jnp.where(own == me, slot, Q), axis=1, keepdims=True)
    code = 2 * jnp.arange(NLON, dtype=jnp.int32)[:, None] + (slot != first).astype(jnp.int32)
    here = dest[None] == me * Q + slot[:, None, None]
    found = jnp.max(jnp.where(here, code[None], 0), axis=(1, 2))
    return jnp.concatenate([one, two, found >> 1, found & 1])


def rows_of(i):
    return pl.ds(pl.multiple_of(i * 8, 8), 8)


def kernel(table, ckpt, kmt, kappa, out_t, out_s,
           blocks, parted, packed, landed, levels, kap, tr, hk,
           east_o, west_o, north_o, south_o, east_i, west_i, north_i, south_i, corner_i,
           vs, col, dep, fresh_t, stream, part, red1, red2,
           in_sem, out_sem, a2a_s, a2a_r, halo_s, halo_r, red_s, red_r):
    lon = lax.axis_index("lon")
    lat = lax.axis_index("lat")
    lon_x, lon_y = lon // SIDE, lon % SIDE
    east, west = (lon + 1) % NLON, (lon + NLON - 1) % NLON
    south, north = (lat + 1) % NLAT, (lat + NLAT - 1) % NLAT

    def peer(k):
        return ((lon_x + k // SIDE) % SIDE) * SIDE + (lon_y + k % SIDE) % SIDE

    loads = [
        pltpu.make_async_copy(ckpt.at[:, pl.ds(g * CHUNK, CHUNK)], blocks.at[:, pl.ds(g * CHUNK, CHUNK)], in_sem.at[g])
        for g in range(5)
    ]
    loads.append(pltpu.make_async_copy(kmt, levels, in_sem.at[5]))
    loads.append(pltpu.make_async_copy(kappa, kap, in_sem.at[6]))
    for load in loads:
        load.start()

    barrier = pltpu.get_barrier_semaphore()
    for k in range(1, NLON):
        pl.semaphore_signal(barrier, inc=1, device_id={"lon": peer(k), "lat": lat})
    for k in range(1, NLAT):
        pl.semaphore_signal(barrier, inc=1, device_id={"lon": lon, "lat": (lat + k) % NLAT})
    for x in (east, west):
        for y in (north, south):
            pl.semaphore_signal(barrier, inc=1, device_id={"lon": x, "lat": y})

    lane = lax.broadcasted_iota(jnp.int32, (8, 128), 1)
    sub = lax.broadcasted_iota(jnp.int32, (8, 128), 0)
    lane32 = lax.broadcasted_iota(jnp.int32, (32, 128), 1)
    lane160 = lax.broadcasted_iota(jnp.int32, (ROWS, 128), 1)
    sub_w = lax.broadcasted_iota(jnp.int32, (8, 512), 0)

    for g in range(5):
        loads[g].wait()
    flat = parted.reshape(Q * ROWS, 128)
    def spread(g, _):
        for r in range(32):
            q, l = divmod(r * BW, 128)
            a = blocks[:, pl.ds(pl.multiple_of(g * CHUNK + q * 128, 128), 128)]
            if l:
                a = pltpu.roll(a, 128 - l, 1)
            if l + BW > 128:
                b = blocks[:, pl.ds(pl.multiple_of(g * CHUNK + q * 128 + 128, 128), 128)]
                a = jnp.where(lane32 < 128 - l, a, pltpu.roll(b, 128 - l, 1))
            flat[pl.ds(g * 32 + r, 32, stride=ROWS), :] = a
        return 0
    lax.fori_loop(0, 5, spread, 0)

    pl.semaphore_wait(barrier, 26)

    def pack(e):
        one = parted[table[e]]
        two = parted[table[NLON + e]]
        return jnp.where(lane160 < 64, one, pltpu.roll(two, 64, 1))

    def block_copy(k):
        return pltpu.make_async_remote_copy(
            src_ref=packed.at[k], dst_ref=landed.at[lon], send_sem=a2a_s.at[k], recv_sem=a2a_r.at[k],
            device_id={"lon": peer(k), "lat": lat})

    def send(k, _):
        packed[k] = pack(peer(k))
        block_copy(k).start()
        return 0
    lax.fori_loop(1, NLON, send, 0)
    landed[lon] = pack(lon)

    loads[5].wait()
    loads[6].wait()
    for i in range(20):
        rows = pl.ds(i * 8, 8)
        for t in range(4):
            w = min(128, COLS - t * 128)
            at = pl.ds(t * 128, w)
            hk[2, rows, at] = levels[rows, at].astype(f32)
            hk[0, rows, at] = kap[0, rows, at]
            hk[1, rows, at] = kap[1, rows, at]

    def halo_copies(h):
        def copy(n, src, dst, x, y):
            return pltpu.make_async_remote_copy(
                src_ref=src, dst_ref=dst, send_sem=halo_s.at[h, n], recv_sem=halo_r.at[h, n],
                device_id={"lon": x, "lat": y})
        low, high = pl.ds(0, 128), pl.ds(384, 128)
        return [
            copy(0, east_o.at[h], west_i.at[h], east, lat),
            copy(1, west_o.at[h], east_i.at[h], west, lat),
            copy(2, north_o.at[h], south_i.at[h], lon, north),
            copy(3, south_o.at[h], north_i.at[h], lon, south),
            copy(4, north_o.at[h, :, :, low], corner_i.at[h, 0], west, north),
            copy(5, north_o.at[h, :, :, high], corner_i.at[h, 1], east, north),
            copy(6, south_o.at[h, :, :, low], corner_i.at[h, 2], west, south),
            copy(7, south_o.at[h, :, :, high], corner_i.at[h, 3], east, south),
        ]

    def stage_halo(h, ref, last):
        for src, tile, start in ((west_o, 0, 0), (east_o, 3, 92)):
            for group in range(3):
                acc = None
                for ii in range(min(8, 20 - group * 8)):
                    i = group * 8 + ii
                    for f in range(4):
                        v = ref[min(f, last), pl.ds(i * 8, 8), pl.ds(tile * 128, 128)]
                        pos = 16 * ii + 4 * f
                        move = (pos - start) % 128
                        v = pltpu.roll(v, move, 1) if move else v
                        acc = v if acc is None else jnp.where(lane >= pos, v, acc)
                src[h, pl.ds(group * 8, 8), :] = acc
        for i in range(2):
            a, b = min(2 * i, last), min(2 * i + 1, last)
            top, bottom = pl.ds(0, 8), pl.ds(152, 8)
            north_o[h, i] = jnp.where(sub_w < 4, ref[a, top, :], pltpu.roll(ref[b, top, :], 4, 0))
            south_o[h, i] = jnp.where(sub_w < 4, pltpu.roll(ref[a, bottom, :], 4, 0), ref[b, bottom, :])

    def unpack_halo(h, ref, last):
        outer = pl.ds(384, 128)
        for i in range(20):
            rows = pl.ds(i * 8, 8)
            from_e = east_i[h, pl.ds((i // 8) * 8, 8), :]
            from_w = west_i[h, pl.ds((i // 8) * 8, 8), :]
            for f in range(last + 1):
                pos = 16 * (i % 8) + 4 * f
                e = pltpu.roll(from_e, (96 - pos) % 128, 1) if pos != 96 else from_e
                w = pltpu.roll(from_w, (124 - pos) % 128, 1) if pos != 124 else from_w
                own = ref[f, rows, outer]
                ref[f, rows, outer] = jnp.where(lane < 96, own, jnp.where(lane < 112, e, w))
        for f in range(last + 1):
            i, odd = divmod(f, 2)
            s, n = south_i[h, i], north_i[h, i]
            se, sw, ne, nw = (corner_i[h, c, i] for c in range(4))
            if odd:
                s, se, sw = (pltpu.roll(v, 4, 0) for v in (s, se, sw))
            else:
                n, ne, nw = (pltpu.roll(v, 4, 0) for v in (n, ne, nw))
            ref[f, pl.ds(160, 8), :] = jnp.where(sub_w < 4, s, n)
            e = pltpu.roll(jnp.where(sub < 4, se, ne), 96, 1)
            w = pltpu.roll(jnp.where(sub < 4, sw, nw), 32, 1)
            mid = ref[f, pl.ds(160, 8), outer]
            ref[f, pl.ds(160, 8), outer] = jnp.where(lane < 96, mid, jnp.where(lane < 112, e, w))

    stage_halo(0, hk, 2)
    early = halo_copies(0)
    for c in early:
        c.start()
    for c in early:
        c.wait_recv()
    unpack_halo(0, hk, 2)
    inside_s = (lat != NLAT - 1).astype(f32)
    inside_n = (lat != 0).astype(f32)
    edge = hk[2, pl.ds(160, 8), :]
    hk[2, pl.ds(160, 8), :] = jnp.where(sub_w < 4, edge * inside_s, edge * inside_n)

    for k in range(1, NLON):
        block_copy(k).wait_recv()

    def place(n, _):
        f, by = n // BY, n % BY
        level = (f % 2).astype(f32)
        src = [table[2 * NLON + by * BX + bx] for bx in range(BX)]
        second = [jnp.full((8, 128), table[2 * NLON + Q + by * BX + bx], jnp.int32) == 1 for bx in range(BX)]
        for i in range(5):
            rows_in = pl.ds(pl.multiple_of(f * BH + i * 8, 8), 8)
            rows_out = pl.ds(pl.multiple_of(by * BH + i * 8, 8), 8)
            v = []
            for bx in range(BX):
                a = landed[src[bx], rows_in, :]
                o = (BW * bx) % 128
                direct = pltpu.roll(a, o, 1) if o else a
                crossed = pltpu.roll(a, (o + 64) % 128, 1) if (o + 64) % 128 else a
                v.append(jnp.where(second[bx], crossed, direct))
            for t, (x, y, z, p, q) in enumerate(((0, 1, 2, 60, 120), (2, 3, 4, 52, 112), (4, 5, 6, 44, 104), (6, 7, 7, 36, 128))):
                at = pl.ds(t * 128, 128)
                w = jnp.where(lane < p, v[x], jnp.where(lane < q, v[y], v[z]))
                tr[f, rows_out, at] = jnp.where(hk[2, rows_out, at] > level, w, 0.0)
        return 0
    lax.fori_loop(0, 16, place, 0)

    stage_halo(1, tr, 3)
    late = halo_copies(1)
    for c in late:
        c.start()
    for c in late:
        c.wait_recv()
    unpack_halo(1, tr, 3)

    def up(c, p):
        return pltpu.roll(jnp.where(sub_w == 7, p, c), 1, 0)

    def down(c, n):
        return pltpu.roll(jnp.where(sub_w == 0, n, c), 7, 0)

    def to_east(c):
        return pltpu.roll(c, 511, 1)

    def to_west(c):
        return pltpu.roll(c, 1, 1)

    def around(i):
        return rows_of(i), rows_of((i + TILES - 1) % TILES), rows_of((i + 1) % TILES)

    def step(i, store):
        here, prev, after = around(i)
        kc = hk[2, here, :]
        ku, kd, ke = up(kc, hk[2, prev, :]), down(kc, hk[2, after, :]), to_east(kc)
        forcing = None
        depth = None
        for l in range(2):
            wet = (kc > l).astype(f32)
            c = hk[l, here, :]
            ge = jnp.where(jnp.minimum(kc, ke) > l, 0.5 * (c + to_east(c)), 0.0)
            gu = jnp.where(jnp.minimum(kc, ku) > l, 0.5 * (c + up(c, hk[l, prev, :])), 0.0)
            gd = jnp.where(jnp.minimum(kc, kd) > l, 0.5 * (c + down(c, hk[l, after, :])), 0.0)
            new = []
            for t in range(2):
                f = 2 * t + l
                c = tr[f, here, :]
                fe = ge * (to_east(c) - c)
                change = fe - to_west(fe) + gd * (down(c, tr[f, after, :]) - c) + gu * (up(c, tr[f, prev, :]) - c)
                v = wet * (c + change)
                new.append(v)
                if store:
                    for part_t in range(4):
                        w = min(128, COLS - part_t * 128)
                        fresh_t[t, l, here, pl.ds(part_t * 128, w)] = v[:, part_t * 128:part_t * 128 + w]
            temp, salt = new
            dens = wet * (haline * salt - thermal * temp - cabbeling * temp * temp)
            dz = 1.0 + 0.5 * l
            forcing = dens if l == 0 else forcing + dz * dens
            depth = wet if l == 0 else depth + dz * wet
        column = (kc > 0).astype(f32)
        col[here, :] = column
        dep[here, :] = depth
        vs[0, here, :] = column * forcing

    def step_own(i, _):
        step(i, True)
        return 0
    lax.fori_loop(0, TILES - 1, step_own, 0)
    result = pltpu.make_async_copy(fresh_t, out_t, out_sem.at[0])
    result.start()
    step(TILES - 1, False)

    sums = []
    for order in range(3):
        def apply(i, acc, order=order, store=True, add=True):
            here, prev, after = around(i)
            c = vs[order, here, :]
            m = up(c, vs[order, prev, :]) + down(c, vs[order, after, :])
            q = c + 0.5 * m
            v = dep[here, :] * c - col[here, :] * (to_east(q) + to_west(q) + m)
            if store:
                vs[order + 1, here, :] = v
            if add:
                acc = (acc[0] + c * c, acc[1] + c * v)
            return acc
        zero = jnp.zeros((8, 512), f32)
        acc = lax.fori_loop(0, TILES - 1, lambda i, a: apply(i, a, store=order < 2), (zero, zero))
        if order < 2:
            apply(TILES - 1, acc, add=False)
        sums += list(acc)

    tile = jnp.zeros((8, 128), f32)
    for k, s in enumerate(sums):
        s = s[:, :128] + s[:, 128:256] + s[:, 256:384] + jnp.where(lane < 96, s[:, 384:], 0.0)
        tile = jnp.where(sub == k, jnp.sum(s, axis=0, keepdims=True), tile)
    part[0] = tile
    red1[lon] = tile

    def red_copy(n, src, dst, x, y):
        return pltpu.make_async_remote_copy(
            src_ref=src, dst_ref=dst, send_sem=red_s.at[n], recv_sem=red_r.at[n], device_id={"lon": x, "lat": y})

    over_lon = [red_copy(k - 1, part.at[0], red1.at[lon], peer(k), lat) for k in range(1, NLON)]
    for c in over_lon:
        c.start()
    for c in over_lon:
        c.wait_recv()
    tile = red1[0]
    for k in range(1, NLON):
        tile = tile + red1[k]
    part[1] = tile
    red2[lat] = tile
    over_lat = [red_copy(14 + k, part.at[1], red2.at[lat], lon, (lat + k) % NLAT) for k in range(1, NLAT)]
    for c in over_lat:
        c.start()
    for c in over_lat:
        c.wait_recv()
    tile = red2[0]
    for k in range(1, NLAT):
        tile = tile + red2[k]
    tile = jnp.sum(tile, axis=1, keepdims=True)
    nu = [tile[k:k + 1] for k in range(6)]

    def dot(a, b):
        total = None
        for i, x in enumerate(a):
            for j, y in enumerate(b):
                term = x * y * nu[i + j]
                total = term if total is None else total + term
        return total

    def image(a):
        return [SHIFT * a[0]] + [SHIFT * a[k] + a[k - 1] for k in range(1, len(a))] + [a[-1]]

    one = jnp.ones((1, 1), f32)
    x = []
    res, direct, norm = [one], [one], nu[0]
    for k in range(3):
        img = image(direct)
        alpha = norm / dot(direct, img)
        x = [(x[n] + alpha * d) if n < len(x) else alpha * d for n, d in enumerate(direct)]
        if k < 2:
            res = [(res[n] - alpha * d) if n < len(res) else -alpha * d for n, d in enumerate(img)]
            later = dot(res, res)
            beta = later / norm
            direct = [(res[n] + beta * direct[n]) if n < len(direct) else res[n] for n in range(len(res))]
            norm = later

    c0, c1, c2 = (jnp.broadcast_to(v, (8, 128)) for v in x)
    for i in range(20):
        rows = pl.ds(i * 8, 8)
        for t in range(4):
            w = min(128, COLS - t * 128)
            at = pl.ds(t * 128, 128)
            v = c0 * vs[0, rows, at] + c1 * vs[1, rows, at] + c2 * vs[2, rows, at]
            stream[rows, pl.ds(t * 128, w)] = v[:, :w]
    final = pltpu.make_async_copy(stream, out_s, out_sem.at[1])
    final.start()

    for k in range(1, NLON):
        block_copy(k).wait_send()
    for c in early + late + over_lon + over_lat:
        c.wait_send()
    result.wait()
    final.wait()


def body(checkpoint, slot_dest, kmt, kappa):
    table = owners(slot_dest[0], lax.axis_index("lon"))
    sem = pltpu.SemaphoreType.DMA
    vm = pltpu.VMEM
    return pl.pallas_call(
        kernel,
        out_shape=(jax.ShapeDtypeStruct((2, 2, ROWS, COLS), f32), jax.ShapeDtypeStruct((ROWS, COLS), f32)),
        in_specs=[pl.BlockSpec(memory_space=pltpu.SMEM)] + [pl.BlockSpec(memory_space=pl.ANY)] * 3,
        out_specs=[pl.BlockSpec(memory_space=pl.ANY)] * 2,
        scratch_shapes=[
            vm((Q, 9600), f32),
            vm((Q, ROWS, 128), f32),
            vm((NLON, ROWS, 128), f32),
            vm((NLON, ROWS, 128), f32),
            vm((ROWS, COLS), jnp.int32),
            vm((2, ROWS, COLS), f32),
            vm((4, TILES * 8, 512), f32),
            vm((3, TILES * 8, 512), f32),
            vm((2, 24, 128), f32),
            vm((2, 24, 128), f32),
            vm((2, 2, 8, 512), f32),
            vm((2, 2, 8, 512), f32),
            vm((2, 24, 128), f32),
            vm((2, 24, 128), f32),
            vm((2, 2, 8, 512), f32),
            vm((2, 2, 8, 512), f32),
            vm((2, 4, 2, 8, 128), f32),
            vm((3, TILES * 8, 512), f32),
            vm((TILES * 8, 512), f32),
            vm((TILES * 8, 512), f32),
            vm((2, 2, ROWS, COLS), f32),
            vm((ROWS, COLS), f32),
            vm((2, 8, 128), f32),
            vm((NLON, 8, 128), f32),
            vm((NLAT, 8, 128), f32),
            sem((7,)),
            sem((2,)),
            sem((NLON,)),
            sem((NLON,)),
            sem((2, 8)),
            sem((2, 8)),
            sem((22,)),
            sem((22,)),
        ],
        compiler_params=pltpu.CompilerParams(collective_id=0, has_side_effects=True, vmem_limit_bytes=48 << 20),
    )(table, checkpoint[0], kmt, kappa)


def solution(mesh):
    placed = (P("lat", "lon", None), P("lat", None), P("lat", "lon"), P(None, "lat", "lon"))
    return jax.shard_map(
        body,
        mesh=mesh,
        in_specs=placed,
        out_specs=(P(None, None, "lat", "lon"), P("lat", "lon")),
        check_vma=False,
    )
```

time: 589 us -> 69.3 us (0.12)
  blocking collectives: 323 us -> 0 us
  waiting for transfers between devices: 150 us -> 0 us
  Pallas kernels: 0 us -> 60.1 us
  starting transfers between devices: 43.6 us -> 0 us
  local copies, waits for them, and re-layouts: 36.8 us -> 5.74 us
  between operations: 20.9 us -> 0.67 us
  other arithmetic: 14 us -> 2.48 us
    psum x5 -> x0, blocking collectives: 323 us -> none  [the longest x3 193 us: squares(): return lax.psum(jnp.sum(residual * residual), ('lon', 'lat'))]
    all_gather x1 -> x0, waiting for transfers between devices: 131 us -> none  [body(): lax.all_gather(blocks, 'lon', axis=0, tiled=True)]
    pallas_call x0 -> x1, Pallas kernels: none -> 60.1 us  [body(): pl.pallas_call(kernel, out_shape=(jax.ShapeDtypeStruct((2, 2, ROWS, COLS)...]
    ppermute x16 -> x0, starting transfers between devices: 43.5 us -> none  [the longest x8 26.9 us: extended(): after = lax.ppermute(initial, axis, down)]
    scatter x1 -> x0, local copies, waits for them, and re-layouts: 18.8 us -> none  [body(): empty.at[target].set(lax.all_gather(blocks, 'lon', axis=0, tiled=True))]
    ppermute x16 -> x0, waiting for transfers between devices: 18.4 us -> none  [the longest x8 9.51 us: extended(): before = lax.ppermute(last, axis, up)]
    reshape x3 -> x0, local copies, waits for them, and re-layouts: 10.1 us -> none  [the longest x1 5.43 us: body(): field = placed.reshape(block_rows, block_cols, 2, LEV, BH, BW)]
  transfers between devices with their start and end apart: 17 -> 0, of which waited for: 9 -> 0; matrix products, arithmetic and copies ran while one was open for 1% -> 0% of each run, Pallas kernels for 0% -> 0%
where the time goes in v1:
time: 69.3 us; the launch traced here: 69 us
  Pallas kernels  60.1 us (87%)
  local copies, waits for them, and re-layouts  5.74 us (8%)
  other arithmetic  2.48 us (4%)
    pallas_call x1, Pallas kernels, body(): pl.pallas_call(kernel, out_shape=(jax.ShapeDtypeStruct((2, 2, ROWS, COLS)...  60.1 us
    unnamed x9, local copies, waits for them, and re-layouts  5.65 us

profile of v1, /device:TPU:1, one launch (start us, length us, event | category | flops | bytes accessed | tf_op | source)
XLA Modules:
  0.0 69.0 jit_solution(6581043492225746927)
XLA Ops:
  0.7 0.5 broadcast.65
  1.2 1.3 %reduce.3 = s32[512]{0:T(512)S(1)} reduce(s32[1,512]{1,0:T(1,128)} %param.5, s32[]{:T(128)} %broadcast.65), dimensions={0}, to_apply=%param.5.reduce_sub_computation.3 | reduce | bytes 4100 | tf_op args[1]
  2.5 0.1 reshape_squeeze.3
  2.6 0.1 broadcast_shift-right-arithmetic_fusion
  2.7 0.1 select_reduce_fusion.3
  2.8 0.1 convert_add_fusion
  2.9 0.7 %select_reduce_fusion = s32[32]{0:T(128)S(1)} fusion(s32[16,32]{1,0:T(8,128)S(1)} %convert_add_fusion, s32[16,32]{1,0:T(8,128)S(1)} %reshape_squeeze.3, s32[32]{0:T(128)S(1)} %iota_add_fusion), kind=kLoop, calls=%fused_computation | loop fusion | flops 49120 | bytes 4352 | tf_op jit(solution)/shard_map/reduce_max | solution.py:40
  3.7 0.1 pad_add_fusion.table
  3.7 0.0 copy-start
  3.8 1.3 %copy-done = f32[1,32,9600]{2,1,0:T(8,128)S(1)} copy-done((f32[1,32,9600]{2,1,0:T(8,128)S(1)}, f32[1,32,9600]{2,1,0:T(8,128)}, u32[]{:S(2)}) %copy-start) | copy-done | bytes 1228824
  5.0 0.0 copy-start.1
  5.0 1.1 %copy-done.1 = f32[2,160,480]{2,1,0:T(8,128)S(1)} copy-done((f32[2,160,480]{2,1,0:T(8,128)S(1)}, f32[2,160,480]{2,1,0:T(8,128)}, u32[]{:S(2)}) %copy-start.1) | copy-done | bytes 614424
  6.1 0.0 copy-start.2
  6.1 1.0 %copy-done.2 = s32[160,480]{1,0:T(8,128)S(1)} copy-done((s32[160,480]{1,0:T(8,128)S(1)}, s32[160,480]{1,0:T(8,128)}, u32[]{:S(2)}) %copy-start.2) | copy-done | bytes 307224
  7.1 60.1 %shard_map.59 = (f32[2,2,160,480]{3,2,1,0:T(8,128)S(1)}, f32[160,480]{1,0:T(8,128)S(1)}) custom-call(s32[96]{0:T(128)S(1)} %pad_add_fusion.table, f32[32,9600]{1,0:T(8,128)S(1)} %bitcast.3, s32[160,480]{1,0:T(8,128)S(1)} %copy-done.2, f32[2,160,480]{2,1,0:T(8,128)S(1)} %copy-done.1), custom_call_target="tpu_custom_call" | custom-call | tf_op jit(solution)/shard_map/pallas_call | solution.py:395
  67.2 1.1 %copy.8 = f32[2,2,160,480]{3,2,1,0:T(8,128)} copy(f32[2,2,160,480]{3,2,1,0:T(8,128)S(1)} %get-tuple-element.10) | data formatting | bytes 2457600
  68.3 0.7 %copy.9 = f32[160,480]{1,0:T(8,128)} copy(f32[160,480]{1,0:T(8,128)S(1)} %get-tuple-element.11) | data formatting | bytes 614400
  (4 shorter events, 0.0 us)
Async XLA Ops:
  3.7 1.3 %copy-start = (f32[1,32,9600]{2,1,0:T(8,128)S(1)}, f32[1,32,9600]{2,1,0:T(8,128)}, u32[]{:S(2)}) copy-start(f32[1,32,9600]{2,1,0:T(8,128)} %param.4) | copy-start | bytes 3686404
  5.0 1.1 %copy-start.1 = (f32[2,160,480]{2,1,0:T(8,128)S(1)}, f32[2,160,480]{2,1,0:T(8,128)}, u32[]{:S(2)}) copy-start(f32[2,160,480]{2,1,0:T(8,128)} %kappa.1) | copy-start | bytes 1843204
  6.1 1.0 %copy-start.2 = (s32[160,480]{1,0:T(8,128)S(1)}, s32[160,480]{1,0:T(8,128)}, u32[]{:S(2)}) copy-start(s32[160,480]{1,0:T(8,128)} %kmt.1) | copy-start | bytes 921604

commit v2 on v0

v2 whole, which is shorter than its diff:
```python
import jax
import jax.numpy as jnp
from jax import lax
from jax.experimental import pallas as pl
from jax.experimental.pallas import tpu as pltpu
from jax.sharding import PartitionSpec as P

BW = 60
BH = 40
BX = 8
BY = 4
Q = 32
ROWS = 160
COLS = 480
NLON = 16
NLAT = 8
SIDE = 4
TILES = 21
WIDE = TILES * 8
PART = BH * BW
SHIFT = 6.0
ORDER = (0, 2, 1, 3)
KAPPA, KMT = 4, 6

thermal = 0.25
haline = 0.75
cabbeling = 0.05

f32 = jnp.float32
i32 = jnp.int32


def hops(step):
    return (0, 1, 2, 1)[step]


BAND = [(2, 2), (0, 1), (1, 0), (0, 3), (3, 0), (2, 1), (1, 2), (2, 3), (3, 2), (1, 1), (3, 3), (1, 3), (3, 1), (0, 2), (2, 0)]
EVERY = sorted(
    [(x, y, z, c) for x in range(4) for y in range(4) for z in range(4) for c in range(2) if x or y or z or c],
    key=lambda k: -(hops(k[0]) + hops(k[1]) + hops(k[2])),
)


def kernel(ckpt, dest, kmt, kappa, out_t, out_s,
           blocks, slots, row, table, parted, packed, landed0, landed1, landed2, landed3, levels, kap, al, face,
           strips_o, strips_i, rows_i, corners_i,
           vs, col, dep, fresh_t, stream, part, gathered,
           in_sem, out_sem, a2a_s, a2a_r, halo_s, halo_r, red_s, red_r):
    lon = lax.axis_index("lon")
    lat = lax.axis_index("lat")
    landed = (landed0, landed1, landed2, landed3)
    xs = [lax.rem(lon // SIDE + d, SIDE) * SIDE for d in range(4)]
    ys = [lax.rem(lax.rem(lon, SIDE) + d, SIDE) for d in range(4)]
    zs = [lax.rem(lat // 2 + d, 4) * 2 for d in range(4)]
    cs = [lax.rem(lat + d, 2) for d in range(2)]
    east, west = lax.rem(lon + 1, NLON), lax.rem(lon + NLON - 1, NLON)
    south, north = lax.rem(lat + 1, NLAT), lax.rem(lat + NLAT - 1, NLAT)

    get_slots = pltpu.make_async_copy(dest, slots, in_sem.at[0])
    get_blocks = pltpu.make_async_copy(ckpt, blocks, in_sem.at[1])
    get_kmt = pltpu.make_async_copy(kmt, levels, in_sem.at[2])
    get_kappa = pltpu.make_async_copy(kappa, kap, in_sem.at[3])
    for load in (get_slots, get_blocks, get_kmt, get_kappa):
        load.start()

    barrier = pltpu.get_barrier_semaphore()
    for x, y, z, c in EVERY:
        pl.semaphore_signal(barrier, inc=1, device_id={"lon": xs[x] + ys[y], "lat": zs[z] + cs[c]})

    lane = lax.broadcasted_iota(i32, (8, 128), 1)
    sub = lax.broadcasted_iota(i32, (8, 128), 0)
    lane32 = lax.broadcasted_iota(i32, (32, 128), 1)
    lane40 = lax.broadcasted_iota(i32, (BH, 128), 1)
    sub_w = lax.broadcasted_iota(i32, (8, 512), 0)

    get_slots.wait()
    dst = slots[...]
    owner = dst >> 5
    at = lax.broadcasted_iota(i32, (1, NLON * Q), 1)
    source, slot = at >> 5, at & 31
    count = (owner == lon).astype(i32)
    for d in (1, 2, 4, 8, 16):
        count = count + jnp.where(slot >= d, pltpu.roll(count, d, 1), 0)
    code = 2 * source + jnp.clip(count - 1, 0, 1)
    position = lax.broadcasted_iota(i32, (Q, NLON * Q), 0)
    found = jnp.max(jnp.where(dst == lon * Q + position, code, 0), axis=1, keepdims=True)
    to = jnp.where(source == lon, owner, -1) == lax.broadcasted_iota(i32, (NLON, NLON * Q), 0)
    one = jnp.min(jnp.where(to, slot, Q - 1), axis=1, keepdims=True)
    two = jnp.max(jnp.where(to, slot, 0), axis=1, keepdims=True)
    entries = jnp.concatenate([one, two, found], axis=0)
    diagonal = lax.broadcasted_iota(i32, (64, 128), 0) == lax.broadcasted_iota(i32, (64, 128), 1)
    row[...] = jnp.sum(jnp.where(diagonal, entries, 0), axis=0, keepdims=True)
    to_scalars = pltpu.make_async_copy(row, table, in_sem.at[4])
    to_scalars.start()

    get_blocks.wait()

    def spread(f):
        flat = parted.at[f].reshape(Q * BH, 128)
        for r in range(BH):
            q, l = divmod(f * PART + r * BW, 128)
            a = blocks[:, pl.ds(q * 128, 128)]
            if l:
                a = pltpu.roll(a, 128 - l, 1)
            if l + BW > 128:
                b = blocks[:, pl.ds(q * 128 + 128, 128)]
                a = jnp.where(lane32 < 128 - l, a, pltpu.roll(b, 128 - l, 1))
            flat[pl.ds(r, Q, stride=BH), :] = a

    def pack(f, e):
        a = parted[f, table[0, e]]
        b = parted[f, table[0, NLON + e]]
        return jnp.where(lane40 < 64, a, pltpu.roll(b, 64, 1))

    def send_part(f):
        for k, (x, y) in enumerate(BAND):
            e = xs[x] + ys[y]
            packed[f, k] = pack(f, e)
            pltpu.make_async_remote_copy(
                src_ref=packed.at[f, k], dst_ref=landed[f].at[lon], send_sem=a2a_s.at[f], recv_sem=a2a_r.at[f],
                device_id={"lon": e, "lat": lat}).start()
        landed[f][lon] = pack(f, lon)

    spread(ORDER[0])
    to_scalars.wait()
    pl.semaphore_wait(barrier, len(EVERY))
    for n, f in enumerate(ORDER):
        if n:
            spread(f)
        send_part(f)

    def part_done(sem, f):
        most = landed[f].at[pl.ds(0, NLON - 1)]
        return pltpu.make_async_copy(most, most, sem.at[f])

    def stage_strips(f):
        for side, tile, start in ((0, 3, 92), (1, 0, 0)):
            acc = None
            for i in range(20):
                move = (4 * i - start) % 128
                v = al[f, pl.ds(i * 8, 8), pl.ds(tile * 128, 128)]
                v = pltpu.roll(v, move, 1) if move else v
                acc = v if acc is None else jnp.where(lane >= 4 * i, v, acc)
            strips_o[side, f] = acc

    def start_halo(h, f, n):
        fs = pl.ds(f, n)
        top, bottom, low, high = pl.ds(0, 8), pl.ds(152, 8), pl.ds(0, 128), pl.ds(384, 128)

        def copy(kind, src, dst, x, y):
            pltpu.make_async_remote_copy(
                src_ref=src, dst_ref=dst, send_sem=halo_s.at[h, kind], recv_sem=halo_r.at[h, kind],
                device_id={"lon": x, "lat": y}).start()
        copy(2, al.at[fs, top, low], corners_i.at[0, fs], west, north)
        copy(2, al.at[fs, top, high], corners_i.at[1, fs], east, north)
        copy(2, al.at[fs, bottom, low], corners_i.at[2, fs], west, south)
        copy(2, al.at[fs, bottom, high], corners_i.at[3, fs], east, south)
        copy(0, strips_o.at[0, fs], strips_i.at[0, fs], east, lat)
        copy(0, strips_o.at[1, fs], strips_i.at[1, fs], west, lat)
        copy(1, al.at[fs, top, :], rows_i.at[0, fs], lon, north)
        copy(1, al.at[fs, bottom, :], rows_i.at[1, fs], lon, south)

    def wait_halo(h, f, n):
        fs = pl.ds(f, n)
        for kind, ref in enumerate((strips_i, rows_i, corners_i)):
            for sem in (halo_s, halo_r):
                pltpu.make_async_copy(ref.at[:, fs], ref.at[:, fs], sem.at[h, kind]).wait()

    def unpack_halo(f):
        outer = pl.ds(384, 128)
        from_w, from_e = strips_i[0, f], strips_i[1, f]
        for i in range(20):
            rows = pl.ds(i * 8, 8)
            e = pltpu.roll(from_e, 96 - 4 * i, 1) if i != 24 else from_e
            w = pltpu.roll(from_w, 124 - 4 * i, 1)
            al[f, rows, outer] = jnp.where(lane < 96, al[f, rows, outer], jnp.where(lane < 112, e, w))
        last = jnp.where(sub_w < 4, rows_i[0, f], rows_i[1, f])
        e = pltpu.roll(jnp.where(sub < 4, corners_i[0, f], corners_i[2, f]), 96, 1)
        w = pltpu.roll(jnp.where(sub < 4, corners_i[1, f], corners_i[3, f]), 32, 1)
        al[f, pl.ds(160, 8), pl.ds(0, 384)] = last[:, :384]
        al[f, pl.ds(160, 8), outer] = jnp.where(lane < 96, last[:, 384:], jnp.where(lane < 112, e, w))

    def rows_of(i):
        return pl.ds(pl.multiple_of(i * 8, 8), 8)

    def around(i):
        return rows_of(i), rows_of(lax.rem(i + TILES - 1, TILES)), rows_of(lax.rem(i + 1, TILES))

    def up(c, p):
        return pltpu.roll(jnp.where(sub_w == 7, p, c), 1, 0)

    def down(c, n):
        return pltpu.roll(jnp.where(sub_w == 0, n, c), 7, 0)

    def to_east(c):
        return pltpu.roll(c, 511, 1)

    def to_west(c):
        return pltpu.roll(c, 1, 1)

    get_kmt.wait()
    get_kappa.wait()

    def widen(i, _):
        rows = rows_of(i)
        for t in range(4):
            w = min(128, COLS - t * 128)
            at = pl.ds(t * 128, w)
            al[KMT, rows, at] = levels[rows, at].astype(f32)
            al[KAPPA, rows, at] = kap[0, rows, at]
            al[KAPPA + 1, rows, at] = kap[1, rows, at]
        return 0
    lax.fori_loop(0, 20, widen, 0)
    for f in (4, 5, 6):
        stage_strips(f)
    start_halo(4, 4, 3)
    wait_halo(4, 4, 3)
    for f in (4, 5, 6):
        unpack_halo(f)
    inside_s = (lat != NLAT - 1).astype(f32)
    inside_n = (lat != 0).astype(f32)
    edge = al[KMT, pl.ds(160, 8), :]
    al[KMT, pl.ds(160, 8), :] = jnp.where(sub_w < 4, edge * inside_s, edge * inside_n)

    def faces(i, _):
        here, prev, after = around(i)
        kc = al[KMT, here, :]
        ku, kd, ke = up(kc, al[KMT, prev, :]), down(kc, al[KMT, after, :]), to_east(kc)
        ku, kd, ke = jnp.minimum(kc, ku), jnp.minimum(kc, kd), jnp.minimum(kc, ke)
        for l in range(2):
            c = al[KAPPA + l, here, :]
            face[3 * l, here, :] = jnp.where(ke > l, 0.5 * (c + to_east(c)), 0.0)
            face[3 * l + 1, here, :] = jnp.where(ku > l, 0.5 * (c + up(c, al[KAPPA + l, prev, :])), 0.0)
            face[3 * l + 2, here, :] = jnp.where(kd > l, 0.5 * (c + down(c, al[KAPPA + l, after, :])), 0.0)
        col[here, :] = (kc > 0).astype(f32)
        dep[here, :] = (kc > 0).astype(f32) + 1.5 * (kc > 1).astype(f32)
        return 0
    lax.fori_loop(0, TILES, faces, 0)

    def place(f):
        level = float(f % 2)

        def band(by, _):
            code = [table[0, 32 + by * BX + bx] for bx in range(BX)]
            src = [c >> 1 for c in code]
            second = [jnp.full((8, 128), c & 1, i32) == 1 for c in code]
            for i in range(5):
                rows_out = pl.ds(pl.multiple_of(by * BH + i * 8, 8), 8)
                v = []
                for bx in range(BX):
                    a = landed[f][src[bx], pl.ds(i * 8, 8), :]
                    o = (BW * bx) % 128
                    direct = pltpu.roll(a, o, 1) if o else a
                    crossed = pltpu.roll(a, (o + 64) % 128, 1)
                    v.append(jnp.where(second[bx], crossed, direct))
                for t, (x, y, z, p, q) in enumerate(((0, 1, 2, 60, 120), (2, 3, 4, 52, 112), (4, 5, 6, 44, 104), (6, 7, 7, 36, 128))):
                    at = pl.ds(t * 128, 128)
                    w = jnp.where(lane < p, v[x], jnp.where(lane < q, v[y], v[z]))
                    al[f, rows_out, at] = jnp.where(al[KMT, rows_out, at] > level, w, 0.0)
            return 0
        lax.fori_loop(0, BY, band, 0)

    def diffuse(f, first):
        t, l = divmod(f, 2)
        dz = 1.0 + 0.5 * l

        def tile(i, store):
            here, prev, after = around(i)
            c = al[f, here, :]
            fe = face[3 * l, here, :] * (to_east(c) - c)
            change = fe - to_west(fe)
            change = change + face[3 * l + 1, here, :] * (up(c, al[f, prev, :]) - c)
            change = change + face[3 * l + 2, here, :] * (down(c, al[f, after, :]) - c)
            v = jnp.where(al[KMT, here, :] > float(l), c + change, 0.0)
            if store:
                for p in range(4):
                    w = min(128, COLS - p * 128)
                    fresh_t[t, l, here, pl.ds(p * 128, w)] = v[:, p * 128:p * 128 + w]
            share = (dz * haline) * v if t else (-dz) * (thermal * v + cabbeling * v * v)
            vs[0, here, :] = share if first else vs[0, here, :] + share

        def several(j, _):
            for d in range(2):
                tile(2 * j + d, True)
            return 0
        lax.fori_loop(0, 10, several, 0)
        tile(TILES - 1, False)

    for n, f in enumerate(ORDER):
        part_done(a2a_r, f).wait()
        place(f)
        stage_strips(f)
        start_halo(f, f, 1)
        if n:
            g = ORDER[n - 1]
            wait_halo(g, g, 1)
            unpack_halo(g)
            diffuse(g, n == 1)
    g = ORDER[3]
    wait_halo(g, g, 1)
    unpack_halo(g)
    diffuse(g, False)
    result = pltpu.make_async_copy(fresh_t, out_t, out_sem.at[0])
    result.start()

    sums = []
    for order in range(3):
        def apply(i, acc, order=order, add=True):
            here, prev, after = around(i)
            c = vs[order, here, :]
            m = up(c, vs[order, prev, :]) + down(c, vs[order, after, :])
            q = c + 0.5 * m
            v = dep[here, :] * c - col[here, :] * (to_east(q) + to_west(q) + m)
            if order < 2:
                vs[order + 1, here, :] = v
            return (acc[0] + c * c, acc[1] + c * v) if add else acc

        def several(j, acc, apply=apply):
            for d in range(4):
                acc = apply(4 * j + d, acc)
            return acc
        zero = jnp.zeros((8, 512), f32)
        acc = lax.fori_loop(0, 5, several, (zero, zero))
        if order < 2:
            apply(TILES - 1, acc, add=False)
        sums += list(acc)

    tile = jnp.zeros((8, 128), f32)
    for k, s in enumerate(sums):
        s = s[:, :128] + s[:, 128:256] + s[:, 256:384] + jnp.where(lane < 96, s[:, 384:], 0.0)
        tile = jnp.where(sub == k, jnp.sum(s, axis=0, keepdims=True), tile)
    tile = jnp.where(sub == lane, jnp.sum(tile, axis=1, keepdims=True), 0.0)
    mine = jnp.sum(tile, axis=0, keepdims=True)
    part[...] = mine
    for k, (x, y, z, c) in enumerate(EVERY):
        pltpu.make_async_remote_copy(
            src_ref=part, dst_ref=gathered.at[k], send_sem=red_s, recv_sem=red_r,
            device_id={"lon": xs[x] + ys[y], "lat": zs[z] + cs[c]}).start()
    pltpu.make_async_copy(gathered, gathered, red_r).wait()
    total = mine + jnp.sum(gathered[...], axis=0)
    nu = [total[:, k:k + 1] for k in range(6)]

    def dot(a, b):
        total = None
        for i, x in enumerate(a):
            for j, y in enumerate(b):
                term = x * y * nu[i + j]
                total = term if total is None else total + term
        return total

    def image(a):
        return [SHIFT * a[0]] + [SHIFT * a[k] + a[k - 1] for k in range(1, len(a))] + [a[-1]]

    unit = jnp.ones((1, 1), f32)
    x = []
    res, direct, norm = [unit], [unit], nu[0]
    for k in range(3):
        img = image(direct)
        alpha = norm / dot(direct, img)
        x = [(x[n] + alpha * d) if n < len(x) else alpha * d for n, d in enumerate(direct)]
        if k < 2:
            res = [(res[n] - alpha * d) if n < len(res) else -alpha * d for n, d in enumerate(img)]
            later = dot(res, res)
            beta = later / norm
            direct = [(res[n] + beta * direct[n]) if n < len(direct) else res[n] for n in range(len(res))]
            norm = later

    c0, c1, c2 = (jnp.broadcast_to(v, (8, 128)) for v in x)
    for i in range(20):
        rows = pl.ds(i * 8, 8)
        for t in range(4):
            w = min(128, COLS - t * 128)
            at = pl.ds(t * 128, 128)
            v = c0 * vs[0, rows, at] + c1 * vs[1, rows, at] + c2 * vs[2, rows, at]
            stream[rows, pl.ds(t * 128, w)] = v[:, :w]
    final = pltpu.make_async_copy(stream, out_s, out_sem.at[1])
    final.start()

    for f in ORDER:
        part_done(a2a_s, f).wait()
    pltpu.make_async_copy(gathered, gathered, red_s).wait()
    result.wait()
    final.wait()


def body(checkpoint, slot_dest, kmt, kappa):
    sem = pltpu.SemaphoreType.DMA
    vm = pltpu.VMEM
    return pl.pallas_call(
        kernel,
        out_shape=(jax.ShapeDtypeStruct((2, 2, ROWS, COLS), f32), jax.ShapeDtypeStruct((ROWS, COLS), f32)),
        in_specs=[pl.BlockSpec(memory_space=pl.ANY)] * 4,
        out_specs=[pl.BlockSpec(memory_space=pl.ANY)] * 2,
        scratch_shapes=[
            vm((Q, 9600), f32),
            vm((1, NLON * Q), i32),
            vm((1, 128), i32),
            pltpu.SMEM((1, 128), i32),
            vm((4, Q, BH, 128), f32),
            vm((4, NLON - 1, BH, 128), f32),
            *[vm((NLON, BH, 128), f32)] * 4,
            vm((ROWS, COLS), i32),
            vm((2, ROWS, COLS), f32),
            vm((7, WIDE, 512), f32),
            vm((6, WIDE, 512), f32),
            vm((2, 7, 8, 128), f32),
            vm((2, 7, 8, 128), f32),
            vm((2, 7, 8, 512), f32),
            vm((4, 7, 8, 128), f32),
            vm((3, WIDE, 512), f32),
            vm((WIDE, 512), f32),
            vm((WIDE, 512), f32),
            vm((2, 2, ROWS, COLS), f32),
            vm((ROWS, COLS), f32),
            vm((1, 128), f32),
            vm((NLON * NLAT - 1, 1, 128), f32),
            sem((5,)),
            sem((2,)),
            sem((4,)),
            sem((4,)),
            sem((5, 3)),
            sem((5, 3)),
            sem,
            sem,
        ],
        compiler_params=pltpu.CompilerParams(collective_id=0, has_side_effects=True, vmem_limit_bytes=60 << 20),
    )(checkpoint[0], slot_dest, kmt, kappa)


def solution(mesh):
    placed = (P("lat", "lon", None), P("lat", None), P("lat", "lon"), P(None, "lat", "lon"))
    return jax.shard_map(
        body,
        mesh=mesh,
        in_specs=placed,
        out_specs=(P(None, None, "lat", "lon"), P("lat", "lon")),
        check_vma=False,
    )
```

time: 589 us -> 63.7 us (0.11)
  blocking collectives: 323 us -> 0 us
  waiting for transfers between devices: 150 us -> 0 us
  Pallas kernels: 0 us -> 59.7 us
  starting transfers between devices: 43.6 us -> 0 us
  local copies, waits for them, and re-layouts: 36.8 us -> 3.24 us
  between operations: 20.9 us -> 0.65 us
  other arithmetic: 14 us -> 0 us
    psum x5 -> x0, blocking collectives: 323 us -> none  [the longest x3 193 us: squares(): return lax.psum(jnp.sum(residual * residual), ('lon', 'lat'))]
    all_gather x1 -> x0, waiting for transfers between devices: 131 us -> none  [body(): lax.all_gather(blocks, 'lon', axis=0, tiled=True)]
    pallas_call x0 -> x1, Pallas kernels: none -> 59.7 us  [body(): pl.pallas_call(kernel, out_shape=(jax.ShapeDtypeStruct((2, 2, ROWS, COLS)...]
    ppermute x16 -> x0, starting transfers between devices: 43.5 us -> none  [the longest x8 26.9 us: extended(): after = lax.ppermute(initial, axis, down)]
    scatter x1 -> x0, local copies, waits for them, and re-layouts: 18.8 us -> none  [body(): empty.at[target].set(lax.all_gather(blocks, 'lon', axis=0, tiled=True))]
    ppermute x16 -> x0, waiting for transfers between devices: 18.4 us -> none  [the longest x8 9.51 us: extended(): before = lax.ppermute(last, axis, up)]
    reshape x3 -> x0, local copies, waits for them, and re-layouts: 10.1 us -> none  [the longest x1 5.43 us: body(): field = placed.reshape(block_rows, block_cols, 2, LEV, BH, BW)]
  transfers between devices with their start and end apart: 17 -> 0, of which waited for: 9 -> 0; matrix products, arithmetic and copies ran while one was open for 1% -> 0% of each run, Pallas kernels for 0% -> 0%
where the time goes in v2:
time: 63.7 us; the launch traced here: 63.6 us
  Pallas kernels  59.7 us (94%)
  local copies, waits for them, and re-layouts  3.24 us (5%)
  between operations  0.65 us (1%)
    pallas_call x1, Pallas kernels, body(): pl.pallas_call(kernel, out_shape=(jax.ShapeDtypeStruct((2, 2, ROWS, COLS)...  59.7 us
    unnamed x4, local copies, waits for them, and re-layouts  3.24 us

profile of v2, /device:TPU:1, one launch (start us, length us, event | category | flops | bytes accessed | tf_op | source)
XLA Modules:
  0.0 63.6 jit_solution(7733977165314487555)
XLA Ops:
  0.6 59.7 %shard_map.59 = (f32[2,2,160,480]{3,2,1,0:T(8,128)}, f32[160,480]{1,0:T(8,128)}) custom-call(f32[32,9600]{1,0:T(8,128)} %bitcast.1, s32[1,512]{1,0:T(1,128)} %dest.1, s32[160,480]{1,0:T(8,128)} %kmt.1, f32[2,160,480]{2,1,0:T(8,128)} %kappa.1), custom_call_target="tpu_custom_call" | custom-call | tf_op jit(solution)/shard_map/pallas_call | solution.py:389
  60.3 0.0 copy-start
  60.3 2.5 %copy.8 = f32[2,2,160,480]{3,2,1,0:T(8,128)} copy(f32[2,2,160,480]{3,2,1,0:T(8,128)} %get-tuple-element.4) | data formatting | bytes 2457600
  62.9 0.0 copy-done
  62.9 0.7 %copy.9 = f32[160,480]{1,0:T(8,128)} copy(f32[160,480]{1,0:T(8,128)S(1)} %copy-done) | data formatting | bytes 614400
Async XLA Ops:
  60.3 2.5 %copy-start = (f32[160,480]{1,0:T(8,128)S(1)}, f32[160,480]{1,0:T(8,128)}, u32[]{:S(2)}) copy-start(f32[160,480]{1,0:T(8,128)} %get-tuple-element.5) | copy-start | bytes 921604

commit v3 on v2

--- a/solution.py
+++ b/solution.py
@@ -121,14 +121,6 @@
                 device_id={"lon": e, "lat": lat}).start()
         landed[f][lon] = pack(f, lon)
 
-    spread(ORDER[0])
-    to_scalars.wait()
-    pl.semaphore_wait(barrier, len(EVERY))
-    for n, f in enumerate(ORDER):
-        if n:
-            spread(f)
-        send_part(f)
-
     def part_done(sem, f):
         most = landed[f].at[pl.ds(0, NLON - 1)]
         return pltpu.make_async_copy(most, most, sem.at[f])
@@ -213,7 +205,16 @@
     lax.fori_loop(0, 20, widen, 0)
     for f in (4, 5, 6):
         stage_strips(f)
+    spread(ORDER[0])
+    to_scalars.wait()
+    pl.semaphore_wait(barrier, len(EVERY))
     start_halo(4, 4, 3)
+    send_part(ORDER[0])
+    for f in ORDER[1:]:
+        spread(f)
+        if f == ORDER[1]:
+            send_part(f)
+
     wait_halo(4, 4, 3)
     for f in (4, 5, 6):
         unpack_halo(f)
@@ -291,6 +292,8 @@
         place(f)
         stage_strips(f)
         start_halo(f, f, 1)
+        if n < 2:
+            send_part(ORDER[n + 2])
         if n:
             g = ORDER[n - 1]
             wait_halo(g, g, 1)

time: 63.7 us -> 51.8 us (0.81)
  Pallas kernels: 59.7 us -> 47.8 us
    pallas_call x1, Pallas kernels: 59.7 us -> 47.8 us  [body(): pl.pallas_call(kernel, out_shape=(jax.ShapeDtypeStruct((2, 2, ROWS, COLS)...]
where the time goes in v3:
time: 51.8 us; the launch traced here: 51.7 us
  Pallas kernels  47.8 us (92%)
  local copies, waits for them, and re-layouts  3.24 us (6%)
  between operations  0.65 us (1%)
    pallas_call x1, Pallas kernels, body(): pl.pallas_call(kernel, out_shape=(jax.ShapeDtypeStruct((2, 2, ROWS, COLS)...  47.8 us
    unnamed x4, local copies, waits for them, and re-layouts  3.24 us

profile of v3, /device:TPU:1, one launch (start us, length us, event | category | flops | bytes accessed | tf_op | source)
XLA Modules:
  0.0 51.7 jit_solution(4121227764594404816)
XLA Ops:
  0.6 47.8 %shard_map.59 = (f32[2,2,160,480]{3,2,1,0:T(8,128)}, f32[160,480]{1,0:T(8,128)}) custom-call(f32[32,9600]{1,0:T(8,128)} %bitcast.1, s32[1,512]{1,0:T(1,128)} %dest.1, s32[160,480]{1,0:T(8,128)} %kmt.1, f32[2,160,480]{2,1,0:T(8,128)} %kappa.1), custom_call_target="tpu_custom_call" | custom-call | tf_op jit(solution)/shard_map/pallas_call | solution.py:392
  48.5 0.0 copy-start
  48.5 2.5 %copy.8 = f32[2,2,160,480]{3,2,1,0:T(8,128)} copy(f32[2,2,160,480]{3,2,1,0:T(8,128)} %get-tuple-element.4) | data formatting | bytes 2457600
  51.0 0.0 copy-done
  51.0 0.7 %copy.9 = f32[160,480]{1,0:T(8,128)} copy(f32[160,480]{1,0:T(8,128)S(1)} %copy-done) | data formatting | bytes 614400
Async XLA Ops:
  48.5 2.5 %copy-start = (f32[160,480]{1,0:T(8,128)S(1)}, f32[160,480]{1,0:T(8,128)}, u32[]{:S(2)}) copy-start(f32[160,480]{1,0:T(8,128)} %get-tuple-element.5) | copy-start | bytes 921604

commit v4 on v3

--- a/solution.py
+++ b/solution.py
@@ -41,10 +41,10 @@
 )
 
 
-def kernel(ckpt, dest, kmt, kappa, out_t, out_s,
+def kernel(ckpt, dest, kmt, kappa, out_t, out_v, out_n,
            blocks, slots, row, table, parted, packed, landed0, landed1, landed2, landed3, levels, kap, al, face,
            strips_o, strips_i, rows_i, corners_i,
-           vs, col, dep, fresh_t, stream, part, gathered,
+           vs, col, dep, fresh_t, part, summed, gathered,
            in_sem, out_sem, a2a_s, a2a_r, halo_s, halo_r, red_s, red_r):
     lon = lax.axis_index("lon")
     lat = lax.axis_index("lat")
@@ -173,10 +173,10 @@
         al[f, pl.ds(160, 8), outer] = jnp.where(lane < 96, last[:, 384:], jnp.where(lane < 112, e, w))
 
     def rows_of(i):
-        return pl.ds(pl.multiple_of(i * 8, 8), 8)
+        return pl.ds(i * 8, 8) if isinstance(i, int) else pl.ds(pl.multiple_of(i * 8, 8), 8)
 
     def around(i):
-        return rows_of(i), rows_of(lax.rem(i + TILES - 1, TILES)), rows_of(lax.rem(i + 1, TILES))
+        return rows_of(i), rows_of((i + TILES - 1) % TILES if isinstance(i, int) else lax.rem(i + TILES - 1, TILES)), rows_of((i + 1) % TILES if isinstance(i, int) else lax.rem(i + 1, TILES))
 
     def up(c, p):
         return pltpu.roll(jnp.where(sub_w == 7, p, c), 1, 0)
@@ -202,7 +202,8 @@
             al[KAPPA, rows, at] = kap[0, rows, at]
             al[KAPPA + 1, rows, at] = kap[1, rows, at]
         return 0
-    lax.fori_loop(0, 20, widen, 0)
+    for i in range(20):
+        widen(i, 0)
     for f in (4, 5, 6):
         stage_strips(f)
     spread(ORDER[0])
@@ -236,7 +237,8 @@
         col[here, :] = (kc > 0).astype(f32)
         dep[here, :] = (kc > 0).astype(f32) + 1.5 * (kc > 1).astype(f32)
         return 0
-    lax.fori_loop(0, TILES, faces, 0)
+    for i in range(TILES):
+        faces(i, 0)
 
     def place(f):
         level = float(f % 2)
@@ -246,7 +248,7 @@
             src = [c >> 1 for c in code]
             second = [jnp.full((8, 128), c & 1, i32) == 1 for c in code]
             for i in range(5):
-                rows_out = pl.ds(pl.multiple_of(by * BH + i * 8, 8), 8)
+                rows_out = pl.ds(by * BH + i * 8, 8)
                 v = []
                 for bx in range(BX):
                     a = landed[f][src[bx], pl.ds(i * 8, 8), :]
@@ -259,7 +261,8 @@
                     w = jnp.where(lane < p, v[x], jnp.where(lane < q, v[y], v[z]))
                     al[f, rows_out, at] = jnp.where(al[KMT, rows_out, at] > level, w, 0.0)
             return 0
-        lax.fori_loop(0, BY, band, 0)
+        for by in range(BY):
+            band(by, 0)
 
     def diffuse(f, first):
         t, l = divmod(f, 2)
@@ -281,10 +284,10 @@
             vs[0, here, :] = share if first else vs[0, here, :] + share
 
         def several(j, _):
-            for d in range(2):
-                tile(2 * j + d, True)
+            for d in range(20):
+                tile(20 * j + d, True)
             return 0
-        lax.fori_loop(0, 10, several, 0)
+        several(0, 0)
         tile(TILES - 1, False)
 
     for n, f in enumerate(ORDER):
@@ -319,15 +322,17 @@
             return (acc[0] + c * c, acc[1] + c * v) if add else acc
 
         def several(j, acc, apply=apply):
-            for d in range(4):
-                acc = apply(4 * j + d, acc)
+            for d in range(20):
+                acc = apply(20 * j + d, acc)
             return acc
         zero = jnp.zeros((8, 512), f32)
-        acc = lax.fori_loop(0, 5, several, (zero, zero))
+        acc = several(0, (zero, zero))
         if order < 2:
             apply(TILES - 1, acc, add=False)
         sums += list(acc)
 
+    powers = pltpu.make_async_copy(vs, out_v, out_sem.at[2])
+    powers.start()
     tile = jnp.zeros((8, 128), f32)
     for k, s in enumerate(sums):
         s = s[:, :128] + s[:, 128:256] + s[:, 256:384] + jnp.where(lane < 96, s[:, 384:], 0.0)
@@ -341,6 +346,31 @@
             device_id={"lon": xs[x] + ys[y], "lat": zs[z] + cs[c]}).start()
     pltpu.make_async_copy(gathered, gathered, red_r).wait()
     total = mine + jnp.sum(gathered[...], axis=0)
+    summed[...] = total
+    sums_out = pltpu.make_async_copy(summed, out_n, out_sem.at[1])
+    sums_out.start()
+
+    for f in ORDER:
+        part_done(a2a_s, f).wait()
+    pltpu.make_async_copy(gathered, gathered, red_s).wait()
+    result.wait()
+    powers.wait()
+    sums_out.wait()
+
+
+def finish(made_t, made_v, made_n, out_t, out_s, fresh_t, vs, summed, stream, in_sem, out_sem):
+    get_sums = pltpu.make_async_copy(made_n, summed, in_sem.at[4])
+    get_powers = pltpu.make_async_copy(made_v, vs, in_sem.at[5])
+    cells = [(t, l) for t in range(2) for l in range(2)]
+    ins = [pltpu.make_async_copy(made_t.at[t, l], fresh_t.at[t, l], in_sem.at[2 * t + l]) for t, l in cells]
+    outs = [pltpu.make_async_copy(fresh_t.at[t, l], out_t.at[t, l], out_sem.at[2 * t + l]) for t, l in cells]
+    for load in [get_sums] + ins + [get_powers]:
+        load.start()
+    for load, store in zip(ins, outs):
+        load.wait()
+        store.start()
+    get_sums.wait()
+    total = summed[...]
     nu = [total[:, k:k + 1] for k in range(6)]
 
     def dot(a, b):
@@ -369,6 +399,7 @@
             norm = later
 
     c0, c1, c2 = (jnp.broadcast_to(v, (8, 128)) for v in x)
+    get_powers.wait()
     for i in range(20):
         rows = pl.ds(i * 8, 8)
         for t in range(4):
@@ -376,24 +407,25 @@
             at = pl.ds(t * 128, 128)
             v = c0 * vs[0, rows, at] + c1 * vs[1, rows, at] + c2 * vs[2, rows, at]
             stream[rows, pl.ds(t * 128, w)] = v[:, :w]
-    final = pltpu.make_async_copy(stream, out_s, out_sem.at[1])
+    final = pltpu.make_async_copy(stream, out_s, out_sem.at[4])
     final.start()
-
-    for f in ORDER:
-        part_done(a2a_s, f).wait()
-    pltpu.make_async_copy(gathered, gathered, red_s).wait()
-    result.wait()
+    for store in outs:
+        store.wait()
     final.wait()
 
 
 def body(checkpoint, slot_dest, kmt, kappa):
     sem = pltpu.SemaphoreType.DMA
     vm = pltpu.VMEM
-    return pl.pallas_call(
+    made = pl.pallas_call(
         kernel,
-        out_shape=(jax.ShapeDtypeStruct((2, 2, ROWS, COLS), f32), jax.ShapeDtypeStruct((ROWS, COLS), f32)),
+        out_shape=(
+            jax.ShapeDtypeStruct((2, 2, ROWS, COLS), f32),
+            jax.ShapeDtypeStruct((3, WIDE, 512), f32),
+            jax.ShapeDtypeStruct((1, 128), f32),
+        ),
         in_specs=[pl.BlockSpec(memory_space=pl.ANY)] * 4,
-        out_specs=[pl.BlockSpec(memory_space=pl.ANY)] * 2,
+        out_specs=[pl.BlockSpec(memory_space=pl.ANY)] * 3,
         scratch_shapes=[
             vm((Q, 9600), f32),
             vm((1, NLON * Q), i32),
@@ -414,11 +446,11 @@
             vm((WIDE, 512), f32),
             vm((WIDE, 512), f32),
             vm((2, 2, ROWS, COLS), f32),
-            vm((ROWS, COLS), f32),
+            vm((1, 128), f32),
             vm((1, 128), f32),
             vm((NLON * NLAT - 1, 1, 128), f32),
             sem((5,)),
-            sem((2,)),
+            sem((3,)),
             sem((4,)),
             sem((4,)),
             sem((5, 3)),
@@ -428,6 +460,21 @@
         ],
         compiler_params=pltpu.CompilerParams(collective_id=0, has_side_effects=True, vmem_limit_bytes=60 << 20),
     )(checkpoint[0], slot_dest, kmt, kappa)
+    return pl.pallas_call(
+        finish,
+        out_shape=(jax.ShapeDtypeStruct((2, 2, ROWS, COLS), f32), jax.ShapeDtypeStruct((ROWS, COLS), f32)),
+        in_specs=[pl.BlockSpec(memory_space=pl.ANY)] * 3,
+        out_specs=[pl.BlockSpec(memory_space=pl.ANY)] * 2,
+        scratch_shapes=[
+            vm((2, 2, ROWS, COLS), f32),
+            vm((3, WIDE, 512), f32),
+            vm((1, 128), f32),
+            vm((ROWS, COLS), f32),
+            sem((6,)),
+            sem((5,)),
+        ],
+        compiler_params=pltpu.CompilerParams(vmem_limit_bytes=60 << 20),
+    )(*made)
 
 
 def solution(mesh):

time: 51.8 us -> 45.2 us (0.87)
  Pallas kernels: 47.8 us -> 44.4 us
  local copies, waits for them, and re-layouts: 3.24 us -> 0 us
    pallas_call x1, Pallas kernels: 47.8 us -> 41.9 us  [body(): pl.pallas_call(kernel, out_shape=(jax.ShapeDtypeStruct((2, 2, ROWS, COLS)...]
    unnamed x4 -> x0, local copies, waits for them, and re-layouts: 3.24 us -> none
    pallas_call x0 -> x1, Pallas kernels: none -> 2.5 us  [body(): pl.pallas_call(finish, out_shape=(jax.ShapeDtypeStruct((2, 2, ROWS, COLS)...]
where the time goes in v4:
time: 45.2 us; the launch traced here: 45 us
  Pallas kernels  44.4 us (98%)
  between operations  0.64 us (1%)
    pallas_call x1, Pallas kernels, body(): pl.pallas_call(kernel, out_shape=(jax.ShapeDtypeStruct((2, 2, ROWS, COLS)...  41.9 us
    pallas_call x1, Pallas kernels, body(): pl.pallas_call(finish, out_shape=(jax.ShapeDtypeStruct((2, 2, ROWS, COLS)...  2.5 us

profile of v4, /device:TPU:1, one launch (start us, length us, event | category | flops | bytes accessed | tf_op | source)
XLA Modules:
  0.0 45.0 jit_solution(24955923639353052)
XLA Ops:
  0.6 41.9 %shard_map.59 = (f32[2,2,160,480]{3,2,1,0:T(8,128)}, f32[3,168,512]{2,1,0:T(8,128)}, f32[1,128]{1,0:T(1,128)}) custom-call(f32[32,9600]{1,0:T(8,128)} %bitcast.1, s32[1,512]{1,0:T(1,128)} %dest.1, s32[160,480]{1,0:T(8,128)} %kmt.1, f32[2,160,480]{2,1,0:T(8,128)} %kappa.1), custom_call_target="tpu_custom_call" | custom-call | tf_op jit(solution)/shard_map/pallas_call | solution.py:420
  42.5 2.5 %shard_map.60 = (f32[2,2,160,480]{3,2,1,0:T(8,128)}, f32[160,480]{1,0:T(8,128)}) custom-call(f32[2,2,160,480]{3,2,1,0:T(8,128)} %get-tuple-element.5.made_t, f32[3,168,512]{2,1,0:T(8,128)} %get-tuple-element.6.made_v, f32[1,128]{1,0:T(1,128)} %get-tuple-element.7.made_n), custom_call_target="tpu_custom_call" | custom-call | tf_op jit(solution)/shard_map/pallas_call | solution.py:463

commit v5 on v4

--- a/solution.py
+++ b/solution.py
@@ -34,7 +34,7 @@
     return (0, 1, 2, 1)[step]
 
 
-BAND = [(2, 2), (0, 1), (1, 0), (0, 3), (3, 0), (2, 1), (1, 2), (2, 3), (3, 2), (1, 1), (3, 3), (1, 3), (3, 1), (0, 2), (2, 0)]
+BAND = [(0, 1), (2, 2), (1, 0), (2, 1), (0, 3), (1, 2), (3, 0), (2, 3), (1, 1), (3, 2), (3, 3), (0, 2), (1, 3), (2, 0), (3, 1)]
 EVERY = sorted(
     [(x, y, z, c) for x in range(4) for y in range(4) for z in range(4) for c in range(2) if x or y or z or c],
     key=lambda k: -(hops(k[0]) + hops(k[1]) + hops(k[2])),
@@ -42,12 +42,13 @@
 
 
 def kernel(ckpt, dest, kmt, kappa, out_t, out_v, out_n,
-           blocks, slots, row, table, parted, packed, landed0, landed1, landed2, landed3, levels, kap, al, face,
+           blocks, slots, row, table, parted, packed0, packed1, packed2, packed3, landed0, landed1, landed2, landed3, levels, kap, al, face,
            strips_o, strips_i, rows_i, corners_i,
            vs, col, dep, fresh_t, part, summed, gathered,
            in_sem, out_sem, a2a_s, a2a_r, halo_s, halo_r, red_s, red_r):
     lon = lax.axis_index("lon")
     lat = lax.axis_index("lat")
+    packed = (packed0, packed1, packed2, packed3)
     landed = (landed0, landed1, landed2, landed3)
     xs = [lax.rem(lon // SIDE + d, SIDE) * SIDE for d in range(4)]
     ys = [lax.rem(lax.rem(lon, SIDE) + d, SIDE) for d in range(4)]
@@ -78,17 +79,21 @@
     owner = dst >> 5
     at = lax.broadcasted_iota(i32, (1, NLON * Q), 1)
     source, slot = at >> 5, at & 31
-    count = (owner == lon).astype(i32)
+    line = lax.broadcasted_iota(i32, (8, NLON * Q), 0)
+    count = (owner == jnp.where(line == 0, lon, jnp.where(line == 1, east, west))).astype(i32)
+    slot_8 = lax.broadcasted_iota(i32, (8, NLON * Q), 1) & 31
     for d in (1, 2, 4, 8, 16):
-        count = count + jnp.where(slot >= d, pltpu.roll(count, d, 1), 0)
-    code = 2 * source + jnp.clip(count - 1, 0, 1)
+        count = count + jnp.where(slot_8 >= d, pltpu.roll(count, d, 1), 0)
+    code, code_e, code_w = (2 * source + jnp.clip(count[k:k + 1] - 1, 0, 1) for k in range(3))
     position = lax.broadcasted_iota(i32, (Q, NLON * Q), 0)
     found = jnp.max(jnp.where(dst == lon * Q + position, code, 0), axis=1, keepdims=True)
+    beside = jnp.where(line < 4, east * Q + line * BX, west * Q + (line - 4) * BX + BX - 1)
+    sides = jnp.max(jnp.where(dst == beside, jnp.where(line < 4, code_e, code_w), 0), axis=1, keepdims=True)
     to = jnp.where(source == lon, owner, -1) == lax.broadcasted_iota(i32, (NLON, NLON * Q), 0)
     one = jnp.min(jnp.where(to, slot, Q - 1), axis=1, keepdims=True)
     two = jnp.max(jnp.where(to, slot, 0), axis=1, keepdims=True)
-    entries = jnp.concatenate([one, two, found], axis=0)
-    diagonal = lax.broadcasted_iota(i32, (64, 128), 0) == lax.broadcasted_iota(i32, (64, 128), 1)
+    entries = jnp.concatenate([one, two, found, sides], axis=0)
+    diagonal = lax.broadcasted_iota(i32, (72, 128), 0) == lax.broadcasted_iota(i32, (72, 128), 1)
     row[...] = jnp.sum(jnp.where(diagonal, entries, 0), axis=0, keepdims=True)
     to_scalars = pltpu.make_async_copy(row, table, in_sem.at[4])
     to_scalars.start()
@@ -112,14 +117,32 @@
         b = parted[f, table[0, NLON + e]]
         return jnp.where(lane40 < 64, a, pltpu.roll(b, 64, 1))
 
+    def pack_sides(f, e):
+        e_east, e_west = lax.rem(e + 1, NLON), lax.rem(e + NLON - 1, NLON)
+        picks = [(table[0, e_east], 0), (table[0, NLON + e_east], 0), (table[0, e_west], 56), (table[0, NLON + e_west], 56)]
+        acc = None
+        for i in range(5):
+            for n, (j, start) in enumerate(picks):
+                pos = 16 * i + 4 * n
+                v = parted[f, j, pl.ds(i * 8, 8), :]
+                move = (pos - start) % 128
+                v = pltpu.roll(v, move, 1) if move else v
+                acc = v if acc is None else jnp.where(lane >= pos, v, acc)
+        return acc
+
     def send_part(f):
+        inner = pl.ds(0, BH)
         for k, (x, y) in enumerate(BAND):
-            e = xs[x] + ys[y]
-            packed[f, k] = pack(f, e)
+            e = jnp.where(cs[0] == 0, xs[x] + ys[y], xs[y] + ys[x])
+            packed[f][k, inner, :] = pack(f, e)
+            if f == ORDER[3]:
+                packed[f][k, pl.ds(BH, 8), :] = pack_sides(f, e)
             pltpu.make_async_remote_copy(
-                src_ref=packed.at[f, k], dst_ref=landed[f].at[lon], send_sem=a2a_s.at[f], recv_sem=a2a_r.at[f],
+                src_ref=packed[f].at[k], dst_ref=landed[f].at[lon], send_sem=a2a_s.at[f], recv_sem=a2a_r.at[f],
                 device_id={"lon": e, "lat": lat}).start()
-        landed[f][lon] = pack(f, lon)
+        landed[f][lon, inner, :] = pack(f, lon)
+        if f == ORDER[3]:
+            landed[f][lon, pl.ds(BH, 8), :] = pack_sides(f, lon)
 
     def part_done(sem, f):
         most = landed[f].at[pl.ds(0, NLON - 1)]
@@ -264,6 +287,30 @@
         for by in range(BY):
             band(by, 0)
 
+    def place_sides(f):
+        level = float(f % 2)
+        outer = pl.ds(384, 128)
+        for by in range(BY):
+            both = []
+            for n in range(2):
+                code = table[0, 64 + 4 * n + by]
+                v = landed[f][code >> 1, pl.ds(BH, 8), :]
+                both.append(jnp.where(jnp.full((8, 128), code & 1, i32) == 1, pltpu.roll(v, 124, 1), v))
+            for i in range(5):
+                rows = pl.ds(by * BH + i * 8, 8)
+                e = pltpu.roll(both[0], 96 - 16 * i, 1)
+                w = pltpu.roll(both[1], 116 - 16 * i, 1)
+                v = jnp.where(al[KMT, rows, outer] > level, jnp.where(lane < 112, e, w), 0.0)
+                al[f, rows, outer] = jnp.where(lane < 96, al[f, rows, outer], v)
+
+    def row_copies(f):
+        return [
+            pltpu.make_async_remote_copy(
+                src_ref=al.at[f, pl.ds(start, 8), :], dst_ref=rows_i.at[n, f], send_sem=halo_s.at[f, n], recv_sem=halo_r.at[f, n],
+                device_id={"lon": lon, "lat": to})
+            for n, (start, to) in enumerate(((0, north), (152, south)))
+        ]
+
     def diffuse(f, first):
         t, l = divmod(f, 2)
         dz = 1.0 + 0.5 * l
@@ -292,20 +339,30 @@
 
     for n, f in enumerate(ORDER):
         part_done(a2a_r, f).wait()
-        place(f)
-        stage_strips(f)
-        start_halo(f, f, 1)
         if n < 2:
             send_part(ORDER[n + 2])
-        if n:
-            g = ORDER[n - 1]
+        place(f)
+        if n < 3:
+            stage_strips(f)
+            start_halo(f, f, 1)
+        else:
+            place_sides(f)
+            last = row_copies(f)
+            for c in last:
+                c.start()
+        if n >= 2:
+            g = ORDER[n - 2]
             wait_halo(g, g, 1)
             unpack_halo(g)
-            diffuse(g, n == 1)
-    g = ORDER[3]
-    wait_halo(g, g, 1)
-    unpack_halo(g)
-    diffuse(g, False)
+            diffuse(g, n == 2)
+    wait_halo(ORDER[2], ORDER[2], 1)
+    unpack_halo(ORDER[2])
+    diffuse(ORDER[2], False)
+    for c in last:
+        c.wait()
+    f = ORDER[3]
+    al[f, pl.ds(160, 8), :] = jnp.where(sub_w < 4, rows_i[0, f], rows_i[1, f])
+    diffuse(f, False)
     result = pltpu.make_async_copy(fresh_t, out_t, out_sem.at[0])
     result.start()
 
@@ -432,8 +489,10 @@
             vm((1, 128), i32),
             pltpu.SMEM((1, 128), i32),
             vm((4, Q, BH, 128), f32),
-            vm((4, NLON - 1, BH, 128), f32),
-            *[vm((NLON, BH, 128), f32)] * 4,
+            *[vm((NLON - 1, BH, 128), f32)] * 3,
+            vm((NLON - 1, BH + 8, 128), f32),
+            *[vm((NLON, BH, 128), f32)] * 3,
+            vm((NLON, BH + 8, 128), f32),
             vm((ROWS, COLS), i32),
             vm((2, ROWS, COLS), f32),
             vm((7, WIDE, 512), f32),

time: 45.2 us -> 44.5 us (0.985)
  Pallas kernels: 44.4 us -> 43.7 us
    pallas_call x1, Pallas kernels: 41.9 us -> 41.2 us  [body(): pl.pallas_call(kernel, out_shape=(jax.ShapeDtypeStruct((2, 2, ROWS, COLS)...]
where the time goes in v5:
time: 44.5 us; the launch traced here: 44.4 us
  Pallas kernels  43.7 us (98%)
  between operations  0.64 us (1%)
    pallas_call x1, Pallas kernels, body(): pl.pallas_call(kernel, out_shape=(jax.ShapeDtypeStruct((2, 2, ROWS, COLS)...  41.2 us
    pallas_call x1, Pallas kernels, body(): pl.pallas_call(finish, out_shape=(jax.ShapeDtypeStruct((2, 2, ROWS, COLS)...  2.5 us

profile of v5, /device:TPU:1, one launch (start us, length us, event | category | flops | bytes accessed | tf_op | source)
XLA Modules:
  0.0 44.4 jit_solution(5668509041197019339)
XLA Ops:
  0.6 41.2 %shard_map.59 = (f32[2,2,160,480]{3,2,1,0:T(8,128)}, f32[3,168,512]{2,1,0:T(8,128)}, f32[1,128]{1,0:T(1,128)}) custom-call(f32[32,9600]{1,0:T(8,128)} %bitcast.1, s32[1,512]{1,0:T(1,128)} %dest.1, s32[160,480]{1,0:T(8,128)} %kmt.1, f32[2,160,480]{2,1,0:T(8,128)} %kappa.1), custom_call_target="tpu_custom_call" | custom-call | tf_op jit(solution)/shard_map/pallas_call | solution.py:477
  41.8 2.5 %shard_map.60 = (f32[2,2,160,480]{3,2,1,0:T(8,128)}, f32[160,480]{1,0:T(8,128)}) custom-call(f32[2,2,160,480]{3,2,1,0:T(8,128)} %get-tuple-element.5.made_t, f32[3,168,512]{2,1,0:T(8,128)} %get-tuple-element.6.made_v, f32[1,128]{1,0:T(1,128)} %get-tuple-element.7.made_n), custom_call_target="tpu_custom_call" | custom-call | tf_op jit(solution)/shard_map/pallas_call | solution.py:522

commit v6 on v5

--- a/solution.py
+++ b/solution.py
@@ -34,7 +34,7 @@
     return (0, 1, 2, 1)[step]
 
 
-BAND = [(0, 1), (2, 2), (1, 0), (2, 1), (0, 3), (1, 2), (3, 0), (2, 3), (1, 1), (3, 2), (3, 3), (0, 2), (1, 3), (2, 0), (3, 1)]
+BAND = [(1, 0), (2, 1), (0, 1), (1, 2), (3, 0), (2, 3), (0, 3), (3, 2), (1, 1), (2, 2), (3, 3), (2, 0), (1, 3), (0, 2), (3, 1)]
 EVERY = sorted(
     [(x, y, z, c) for x in range(4) for y in range(4) for z in range(4) for c in range(2) if x or y or z or c],
     key=lambda k: -(hops(k[0]) + hops(k[1]) + hops(k[2])),
@@ -133,7 +133,7 @@
     def send_part(f):
         inner = pl.ds(0, BH)
         for k, (x, y) in enumerate(BAND):
-            e = jnp.where(cs[0] == 0, xs[x] + ys[y], xs[y] + ys[x])
+            e = xs[x] + ys[y]
             packed[f][k, inner, :] = pack(f, e)
             if f == ORDER[3]:
                 packed[f][k, pl.ds(BH, 8), :] = pack_sides(f, e)

time: 44.5 us -> 43.3 us (0.973)
  Pallas kernels: 43.7 us -> 42.6 us
    pallas_call x1, Pallas kernels: 41.2 us -> 40.1 us  [body(): pl.pallas_call(kernel, out_shape=(jax.ShapeDtypeStruct((2, 2, ROWS, COLS)...]
where the time goes in v6:
time: 43.3 us; the launch traced here: 43.2 us
  Pallas kernels  42.6 us (98%)
  between operations  0.64 us (1%)
    pallas_call x1, Pallas kernels, body(): pl.pallas_call(kernel, out_shape=(jax.ShapeDtypeStruct((2, 2, ROWS, COLS)...  40.1 us
    pallas_call x1, Pallas kernels, body(): pl.pallas_call(finish, out_shape=(jax.ShapeDtypeStruct((2, 2, ROWS, COLS)...  2.5 us

profile of v6, /device:TPU:1, one launch (start us, length us, event | category | flops | bytes accessed | tf_op | source)
XLA Modules:
  0.0 43.2 jit_solution(8039064999157913404)
XLA Ops:
  0.6 40.1 %shard_map.59 = (f32[2,2,160,480]{3,2,1,0:T(8,128)}, f32[3,168,512]{2,1,0:T(8,128)}, f32[1,128]{1,0:T(1,128)}) custom-call(f32[32,9600]{1,0:T(8,128)} %bitcast.1, s32[1,512]{1,0:T(1,128)} %dest.1, s32[160,480]{1,0:T(8,128)} %kmt.1, f32[2,160,480]{2,1,0:T(8,128)} %kappa.1), custom_call_target="tpu_custom_call" | custom-call | tf_op jit(solution)/shard_map/pallas_call | solution.py:477
  40.7 2.5 %shard_map.60 = (f32[2,2,160,480]{3,2,1,0:T(8,128)}, f32[160,480]{1,0:T(8,128)}) custom-call(f32[2,2,160,480]{3,2,1,0:T(8,128)} %get-tuple-element.5.made_t, f32[3,168,512]{2,1,0:T(8,128)} %get-tuple-element.6.made_v, f32[1,128]{1,0:T(1,128)} %get-tuple-element.7.made_n), custom_call_target="tpu_custom_call" | custom-call | tf_op jit(solution)/shard_map/pallas_call | solution.py:522

commit v7 on v6

--- a/solution.py
+++ b/solution.py
@@ -263,7 +263,7 @@
     for i in range(TILES):
         faces(i, 0)
 
-    def place(f):
+    def place(f, bands=range(BY)):
         level = float(f % 2)
 
         def band(by, _):
@@ -284,13 +284,13 @@
                     w = jnp.where(lane < p, v[x], jnp.where(lane < q, v[y], v[z]))
                     al[f, rows_out, at] = jnp.where(al[KMT, rows_out, at] > level, w, 0.0)
             return 0
-        for by in range(BY):
+        for by in bands:
             band(by, 0)
 
-    def place_sides(f):
+    def place_sides(f, bands):
         level = float(f % 2)
         outer = pl.ds(384, 128)
-        for by in range(BY):
+        for by in bands:
             both = []
             for n in range(2):
                 code = table[0, 64 + 4 * n + by]
@@ -341,15 +341,19 @@
         part_done(a2a_r, f).wait()
         if n < 2:
             send_part(ORDER[n + 2])
-        place(f)
+        if n < 3:
+            place(f)
         if n < 3:
             stage_strips(f)
             start_halo(f, f, 1)
         else:
-            place_sides(f)
+            place(f, (0, BY - 1))
+            place_sides(f, (0, BY - 1))
             last = row_copies(f)
             for c in last:
                 c.start()
+            place(f, range(1, BY - 1))
+            place_sides(f, range(1, BY - 1))
         if n >= 2:
             g = ORDER[n - 2]
             wait_halo(g, g, 1)

time: 43.3 us -> 43.3 us (level)
  no operation moved by 1% of the time
where the time goes in v7:
time: 43.3 us; the launch traced here: 43.1 us
  Pallas kernels  42.5 us (98%)
  between operations  0.64 us (1%)
    pallas_call x1, Pallas kernels, body(): pl.pallas_call(kernel, out_shape=(jax.ShapeDtypeStruct((2, 2, ROWS, COLS)...  40 us
    pallas_call x1, Pallas kernels, body(): pl.pallas_call(finish, out_shape=(jax.ShapeDtypeStruct((2, 2, ROWS, COLS)...  2.5 us

profile of v7, /device:TPU:1, one launch (start us, length us, event | category | flops | bytes accessed | tf_op | source)
XLA Modules:
  0.0 43.1 jit_solution(2966713840848907462)
XLA Ops:
  0.6 40.0 %shard_map.59 = (f32[2,2,160,480]{3,2,1,0:T(8,128)}, f32[3,168,512]{2,1,0:T(8,128)}, f32[1,128]{1,0:T(1,128)}) custom-call(f32[32,9600]{1,0:T(8,128)} %bitcast.1, s32[1,512]{1,0:T(1,128)} %dest.1, s32[160,480]{1,0:T(8,128)} %kmt.1, f32[2,160,480]{2,1,0:T(8,128)} %kappa.1), custom_call_target="tpu_custom_call" | custom-call | tf_op jit(solution)/shard_map/pallas_call | solution.py:481
  40.6 2.5 %shard_map.60 = (f32[2,2,160,480]{3,2,1,0:T(8,128)}, f32[160,480]{1,0:T(8,128)}) custom-call(f32[2,2,160,480]{3,2,1,0:T(8,128)} %get-tuple-element.5.made_t, f32[3,168,512]{2,1,0:T(8,128)} %get-tuple-element.6.made_v, f32[1,128]{1,0:T(1,128)} %get-tuple-element.7.made_n), custom_call_target="tpu_custom_call" | custom-call | tf_op jit(solution)/shard_map/pallas_call | solution.py:526
